TPU v7x, 32 devices: a whole 2x2x4 slice. The times are simulated.
32 devices in a mesh: energy: 8 (over z, y), atom: 4 (over x, core).
Axes of the slice: x: 2, y: 2, z: 4, core: 2. Of those that a mesh axis runs over, the one named last changes fastest.
Arguments:
- green_blocks: bfloat16 [64, 8, 2, 128, 128], P('atom', 'energy'), may hold values from -3 to 3
- coupling: bfloat16 [64, 3, 2, 128, 128], P('atom'), may hold values from -0.375 to 0.375
- phonon_weight: float32 [2, 64, 2], P(None, 'atom'), may hold values from 0.1 to 1
- offsets: int32 [64, 2], P('atom'), may hold values from 1 to 2, as said below
- bond_atom: int32 [64], P('atom'), may hold values from 0 to 31, as said below
Outputs:
- sigma: bfloat16 [32, 8, 2, 128, 128], P('atom', 'energy')
Inputs may be any that keep to these rules, and one draw needn't show every extreme that they name: For every bond, its 2 modes' offsets are 1, 2, 1 and 2 in some order. `bond_atom`: atoms k * 8 to (k + 1) * 8 - 1 lie on index k of atom. Among the 16 bonds of one index of atom, every index of atom that is named is named by exactly 8 bonds, and one index of atom is named by 8 bonds of every index of atom.
All inputs are finite; a program needn't handle non-finite values.
Results may differ from a plain program's by a relative error of at most 0.0064.
Values may be sent and summed in bfloat16 or wider, within the bound.
No kernel may reach another device: no remote copies, remote signals or barrier semaphores. Data moves between devices by JAX's collectives and lax.ppermute only.
A program may use at most 64 MiB of HBM per device.

v0:
```python
import jax
import jax.numpy as jnp
from jax import lax
from jax.sharding import PartitionSpec as P

A_DEV = 8


def body(green_blocks, coupling, phonon_weight, offsets, bond_atom):
    bond_count = green_blocks.shape[0]
    energy_count = green_blocks.shape[1]
    cycle_size = energy_count * lax.axis_size("energy")
    row_slices = lax.all_to_all(green_blocks, "energy", split_axis=3, concat_axis=1, tiled=True)
    cycle_energy = jnp.arange(cycle_size, dtype=jnp.int32)
    lower_index = (cycle_energy[None, :, None] - offsets[:, None, :]) % cycle_size
    upper_index = (cycle_energy[None, :, None] + offsets[:, None, :]) % cycle_size
    lower_hit = (lower_index[..., None] == cycle_energy).astype(jnp.float32)
    upper_hit = (upper_index[..., None] == cycle_energy).astype(jnp.float32)
    absorb = phonon_weight[0][:, None, :, None]
    emit = phonon_weight[1][:, None, :, None]
    circulant = jnp.sum(absorb * lower_hit + emit * upper_hit, axis=2)
    cycle_mixed = jnp.einsum(
        "bef,bfpxy->bepxy",
        circulant,
        row_slices.astype(jnp.float32),
        precision=lax.Precision.HIGHEST,
    )
    mixed_half = lax.all_to_all(
        cycle_mixed.astype(jnp.bfloat16), "energy", split_axis=1, concat_axis=3, tiled=True
    )
    real_coupling = coupling[:, :, 0]
    imag_coupling = coupling[:, :, 1]
    real_mixed = mixed_half[:, :, 0]
    imag_mixed = mixed_half[:, :, 1]

    def left_mul(first, second):
        return jnp.einsum("bcij,bejk->becik", first, second, preferred_element_type=jnp.float32)

    def right_mul(first, second):
        return jnp.einsum("becij,bckj->beik", first, second, preferred_element_type=jnp.float32)

    left_real = (left_mul(real_coupling, real_mixed) - left_mul(imag_coupling, imag_mixed)).astype(
        jnp.bfloat16
    )
    left_imag = (left_mul(real_coupling, imag_mixed) + left_mul(imag_coupling, real_mixed)).astype(
        jnp.bfloat16
    )
    out_real = right_mul(left_real, real_coupling) - right_mul(left_imag, imag_coupling)
    out_imag = right_mul(left_real, imag_coupling) + right_mul(left_imag, real_coupling)
    bond_self = jnp.stack([out_real, out_imag], axis=2).astype(jnp.bfloat16)
    owner_count = lax.axis_size("atom")
    capacity = max(2, 2 * bond_count // owner_count)
    owner_index = bond_atom // A_DEV
    local_atom = bond_atom % A_DEV
    bond_order = jnp.arange(bond_count, dtype=jnp.int32)
    same_owner = (owner_index[None, :] == owner_index[:, None]) & (
        bond_order[None, :] < bond_order[:, None]
    )
    rank_index = jnp.sum(same_owner.astype(jnp.int32), axis=1)
    slot_index = owner_index * capacity + rank_index
    slot_count = owner_count * capacity
    slot_order = jnp.arange(slot_count, dtype=jnp.int32)
    slot_match = slot_index[None, :] == slot_order[:, None]
    outgoing = jnp.dot(
        slot_match.astype(jnp.bfloat16),
        bond_self.reshape(bond_count, -1),
        preferred_element_type=jnp.float32,
    )
    outgoing = outgoing.astype(jnp.bfloat16).reshape((owner_count, capacity) + bond_self.shape[1:])
    slot_atom = jnp.sum(jnp.where(slot_match, local_atom[None, :] + 1, 0), axis=1) - 1
    slot_atom = slot_atom.reshape(owner_count, capacity)
    incoming, arriving_atom = (
        lax.all_to_all(outgoing, "atom", split_axis=0, concat_axis=0, tiled=True),
        lax.all_to_all(slot_atom, "atom", split_axis=0, concat_axis=0, tiled=True),
    )
    collect = (
        arriving_atom.reshape(-1)[None, :] == jnp.arange(A_DEV, dtype=jnp.int32)[:, None]
    ).astype(jnp.bfloat16)
    sigma = jnp.dot(collect, incoming.reshape(slot_count, -1), preferred_element_type=jnp.float32)
    return sigma.reshape((A_DEV,) + bond_self.shape[1:]).astype(jnp.bfloat16)


def solution(mesh):
    placed = (
        P("atom", "energy", None, None, None),
        P("atom", None, None, None, None),
        P(None, "atom", None),
        P("atom", None),
        P("atom"),
    )
    return jax.shard_map(
        body,
        mesh=mesh,
        in_specs=placed,
        out_specs=P("atom", "energy", None, None, None),
        check_vma=False,
    )
```

profile of v0, /device:TPU:0, one launch (start us, length us, event | category | flops | bytes accessed | tf_op | source)
XLA Modules:
  0.0 115.1 jit_solution(8086603435270566560)
XLA Ops:
  0.0 3.3 %copy.55 = bf16[16,1,2,128,128]{4,2,0,1,3:T(2,128)(2,1)} copy(bf16[16,1,2,128,128]{4,3,2,1,0:T(8,128)(2,1)} %param.5) | data formatting | bytes 2097152 | tf_op args[0]
  3.3 7.3 %all-to-all-start.1 = ((bf16[16,1,2,128,128]{4,2,0,1,3:T(2,128)(2,1)}), bf16[16,1,2,128,128]{4,2,0,1,3:T(2,128)(2,1)S(1)}, u32[]{:S(2)}, u32[]{:S(2)}) async-start(bf16[16,1,2,128,128]{4,2,0,1,3:T(2,128)(2,1)} %copy.55), calls=%async_computation.1 | async-start | bytes 2097152 | tf_op jit(solution)/shard_map/all_to_all | solution.py:13
  10.8 25.6 %all-to-all-done.1 = bf16[16,1,2,128,128]{4,2,0,1,3:T(2,128)(2,1)S(1)} async-done(((bf16[16,1,2,128,128]{4,2,0,1,3:T(2,128)(2,1)}), bf16[16,1,2,128,128]{4,2,0,1,3:T(2,128)(2,1)S(1)}, u32[]{:S(2)}, u32[]{:S(2)}) %all-to-all-start.1) | async-done | bytes 1048608 | tf_op jit(solution)/shard_map/all_to_all | solution.py:13
  36.4 1.4 %convolution_convert_fusion.1 = bf16[16,8,2,16,128]{4,1,3,2,0:T(8,128)(2,1)S(1)} fusion(f32[16,8,8,1,1]{2,1,4,3,0:T(8,128)S(1)} %copy.73, bf16[16,1,2,8,16,128]{5,2,0,4,3,1:T(2,128)(2,1)S(1)} %bitcast.175), kind=kOutput, calls=%fused_computation.23 | convolution fusion | flops 50855936 | bytes 2101248 | tf_op jit(solution)/shard_map/bef,bfpxy->bepxy/dot_general | solution.py:22
  37.8 1.2 %copy.59 = bf16[16,8,2,16,128]{4,3,2,0,1:T(8,128)(2,1)} copy(bf16[16,8,2,16,128]{4,1,3,2,0:T(8,128)(2,1)S(1)} %convolution_convert_fusion.1) | data formatting | bytes 2097152 | tf_op jit(solution)/shard_map/convert_element_type | solution.py:29
  39.0 4.5 %all-to-all-start.2 = ((bf16[16,8,2,16,128]{4,3,2,0,1:T(8,128)(2,1)}), bf16[16,8,2,16,128]{4,3,2,0,1:T(8,128)(2,1)}, u32[]{:S(2)}, u32[]{:S(2)}) async-start(bf16[16,8,2,16,128]{4,3,2,0,1:T(8,128)(2,1)} %copy.59), calls=%async_computation.2 | async-start | bytes 2097152 | tf_op jit(solution)/shard_map/all_to_all | solution.py:28
  43.8 0.7 sub.40
  44.4 24.6 %all-to-all-done.2 = bf16[16,8,2,16,128]{4,3,2,0,1:T(8,128)(2,1)} async-done(((bf16[16,8,2,16,128]{4,3,2,0,1:T(8,128)(2,1)}), bf16[16,8,2,16,128]{4,3,2,0,1:T(8,128)(2,1)}, u32[]{:S(2)}, u32[]{:S(2)}) %all-to-all-start.2) | async-done | bytes 1048608 | tf_op jit(solution)/shard_map/all_to_all | solution.py:28
  69.1 3.2 %all-to-all-start = ((s32[4,1,8]{2,1,0:T(1,128)}), s32[4,1,8]{2,1,0:T(1,128)S(1)}, u32[]{:S(2)}, u32[]{:S(2)}) async-start(s32[4,1,8]{2,1,0:T(1,128)} %bitcast), calls=%async_computation | async-start | bytes 4096 | tf_op jit(solution)/shard_map/all_to_all | solution.py:74
  72.3 1.5 %copy.60 = bf16[16,8,2,16,128]{4,3,1,2,0:T(8,128)(2,1)S(1)} copy(bf16[16,8,2,16,128]{4,3,2,0,1:T(8,128)(2,1)} %all-to-all-done.2) | data formatting | bytes 2097152 | tf_op jit(solution)/shard_map/all_to_all | solution.py:28
  73.8 0.8 fusion.14
  74.6 0.8 fusion.10
  75.4 0.8 subtract_convert_fusion
  76.3 0.8 fusion.20
  77.1 0.8 add_convert_fusion
  77.9 0.8 fusion.25
  78.7 0.8 fusion.68
  79.5 0.8 fusion.63
  81.0 2.1 %convolution_convert_fusion = bf16[32,32768]{1,0:T(8,128)(2,1)} fusion(bf16[16,32768]{1,0:T(8,128)(2,1)S(1)} %convert_element_type.53, s32[16]{0:T(128)S(1)} %multiply_add_fusion), kind=kOutput, calls=%fused_computation | convolution fusion | flops 34603520 | bytes 3145792 | tf_op jit(solution)/shard_map/dot_general | solution.py:64
  83.2 3.6 %all-to-all-start.3 = ((bf16[4,8,1,2,128,128]{5,1,4,3,2,0:T(8,128)(2,1)}), bf16[4,8,1,2,128,128]{5,1,4,3,2,0:T(8,128)(2,1)S(1)}, u32[]{:S(2)}, u32[]{:S(2)}) async-start(bf16[4,8,1,2,128,128]{5,1,4,3,2,0:T(8,128)(2,1)} %bitcast.47), calls=%async_computation.3 | async-start | bytes 4194304 | tf_op jit(solution)/shard_map/all_to_all | solution.py:73
  87.3 0.7 reduce.3
  88.1 24.4 %all-to-all-done.3 = bf16[4,8,1,2,128,128]{5,1,4,3,2,0:T(8,128)(2,1)S(1)} async-done(((bf16[4,8,1,2,128,128]{5,1,4,3,2,0:T(8,128)(2,1)}), bf16[4,8,1,2,128,128]{5,1,4,3,2,0:T(8,128)(2,1)S(1)}, u32[]{:S(2)}, u32[]{:S(2)}) %all-to-all-start.3) | async-done | bytes 2097184 | tf_op jit(solution)/shard_map/all_to_all | solution.py:73
  113.0 1.2 %fusion.73 = bf16[8,1,2,128,128]{4,0,3,2,1:T(8,128)(2,1)S(1)} fusion(bf16[2,128,128,32]{2,1,0,3:T(8,128)(2,1)S(1)} %bitcast.174, s32[32]{0:T(128)S(1)} %eq.78), kind=kOutput, calls=%fused_computation.35 | convolution fusion | flops 17039616 | bytes 2621568 | tf_op jit(solution)/shard_map/dot_general | solution.py:79
  114.2 0.9 copy.72
  (24 shorter events, 2.2 us)
Async XLA Ops:
  0.0 10.6 %copy-start.1 = (f32[2,16,2]{1,2,0:T(2,128)S(1)}, f32[2,16,2]{1,2,0:T(2,128)}, u32[]{:S(2)}) copy-start(f32[2,16,2]{1,2,0:T(2,128)} %param.7) | copy-start | bytes 772
  0.0 10.6 %copy-start.2 = (s32[16,2]{0,1:T(2,128)S(1)}, s32[16,2]{0,1:T(2,128)}, u32[]{:S(2)}) copy-start(s32[16,2]{0,1:T(2,128)} %param.8) | copy-start | bytes 388
  3.3 33.0 %all-to-all-start.1 = ((bf16[16,1,2,128,128]{4,2,0,1,3:T(2,128)(2,1)}), bf16[16,1,2,128,128]{4,2,0,1,3:T(2,128)(2,1)S(1)}, u32[]{:S(2)}, u32[]{:S(2)}) async-start(bf16[16,1,2,128,128]{4,2,0,1,3:T(2,128)(2,1)} %copy.55), calls=%async_computation.1 | async-start | bytes 2097152 | tf_op jit(solution)/shard_map/all_to_all | solution.py:13
  37.7 5.7 %copy-start.3 = (s32[16]{0:T(128)S(1)}, s32[16]{0:T(128)}, u32[]{:S(2)}) copy-start(s32[16]{0:T(128)} %param.9) | copy-start | bytes 196
  39.0 34.9 %copy-start = (bf16[16,3,2,128,128]{4,3,2,1,0:T(8,128)(2,1)S(1)}, bf16[16,3,2,128,128]{4,3,2,1,0:T(8,128)(2,1)}, u32[]{:S(2)}) copy-start(bf16[16,3,2,128,128]{4,3,2,1,0:T(8,128)(2,1)} %param.6) | copy-start | bytes 9437188
  39.0 30.1 %all-to-all-start.2 = ((bf16[16,8,2,16,128]{4,3,2,0,1:T(8,128)(2,1)}), bf16[16,8,2,16,128]{4,3,2,0,1:T(8,128)(2,1)}, u32[]{:S(2)}, u32[]{:S(2)}) async-start(bf16[16,8,2,16,128]{4,3,2,0,1:T(8,128)(2,1)} %copy.59), calls=%async_computation.2 | async-start | bytes 2097152 | tf_op jit(solution)/shard_map/all_to_all | solution.py:28
  69.1 14.1 %all-to-all-start = ((s32[4,1,8]{2,1,0:T(1,128)}), s32[4,1,8]{2,1,0:T(1,128)S(1)}, u32[]{:S(2)}, u32[]{:S(2)}) async-start(s32[4,1,8]{2,1,0:T(1,128)} %bitcast), calls=%async_computation | async-start | bytes 4096 | tf_op jit(solution)/shard_map/all_to_all | solution.py:74
  83.2 29.3 %all-to-all-start.3 = ((bf16[4,8,1,2,128,128]{5,1,4,3,2,0:T(8,128)(2,1)}), bf16[4,8,1,2,128,128]{5,1,4,3,2,0:T(8,128)(2,1)S(1)}, u32[]{:S(2)}, u32[]{:S(2)}) async-start(bf16[4,8,1,2,128,128]{5,1,4,3,2,0:T(8,128)(2,1)} %bitcast.47), calls=%async_computation.3 | async-start | bytes 4194304 | tf_op jit(solution)/shard_map/all_to_all | solution.py:73
where the time goes:
time: 115 us
  waiting for transfers between devices  74.6 us (65%)
  starting transfers between devices  18.6 us (16%)
  matrix products  11.2 us (10%)
  local copies, waits for them, and re-layouts  9.37 us (8%)
    all_to_all x1, waiting for transfers between devices, body(): lax.all_to_all(green_blocks, 'energy', split_axis=3, concat_axis=1, tiled...  25.6 us
    all_to_all x1, waiting for transfers between devices, body(): lax.all_to_all(cycle_mixed.astype(jnp.bfloat16), 'energy', split_axis=1,...  24.6 us
    all_to_all x1, waiting for transfers between devices, body(): lax.all_to_all(outgoing, 'atom', split_axis=0, concat_axis=0, tiled=True)  24.4 us
    all_to_all x1, starting transfers between devices, body(): lax.all_to_all(green_blocks, 'energy', split_axis=3, concat_axis=1, tiled...  7.28 us
    all_to_all x1, starting transfers between devices, body(): lax.all_to_all(cycle_mixed.astype(jnp.bfloat16), 'energy', split_axis=1,...  4.5 us
    unnamed x10, local copies, waits for them, and re-layouts  3.79 us
    all_to_all x1, starting transfers between devices, body(): lax.all_to_all(outgoing, 'atom', split_axis=0, concat_axis=0, tiled=True)  3.61 us
    dot_general x4, matrix products, right_mul(): jnp.einsum('becij,bckj->beik', first, second, preferred_element_type=jnp....  3.23 us
  transfers between devices with their start and end apart: 4, of which 3 were waited for; matrix products, arithmetic and copies ran while one was open for 11% of the time, Pallas kernels for 0%

commit v1 on v0

v1 whole, which is shorter than its diff:
```python
import functools

import jax
import jax.numpy as jnp
from jax import lax
from jax.experimental import pallas as pl
from jax.experimental.pallas import tpu as pltpu
from jax.sharding import PartitionSpec as P

A_DEV = 8
CHUNKS = 1


def product_kernel(first_row, rows, group, capacity, place_ref, green_ref, coupling_ref, *out_refs):
    step = pl.program_id(0)
    components = coupling_ref.shape[1]
    for index in range(group):
        real_green = green_ref[index, 0, 0]
        imag_green = green_ref[index, 0, 1]
        right = jnp.concatenate(
            [
                jnp.concatenate([real_green, imag_green], axis=1),
                jnp.concatenate([-imag_green, real_green], axis=1),
            ],
            axis=0,
        )
        taken = pl.ds(first_row, rows)
        left = jnp.concatenate(
            [
                jnp.concatenate(
                    [coupling_ref[index, c, 0, taken], coupling_ref[index, c, 1, taken]], axis=1
                )
                for c in range(components)
            ],
            axis=0,
        )
        product = jnp.dot(left, right, preferred_element_type=jnp.float32).astype(jnp.bfloat16)
        total = None
        for c in range(components):
            real_part = coupling_ref[index, c, 0]
            imag_part = coupling_ref[index, c, 1]
            last = jnp.concatenate(
                [
                    jnp.concatenate([real_part, -imag_part], axis=1),
                    jnp.concatenate([imag_part, real_part], axis=1),
                ],
                axis=0,
            )
            term = lax.dot_general(
                product[c * rows : (c + 1) * rows],
                last,
                (((1,), (1,)), ((), ())),
                preferred_element_type=jnp.float32,
            )
            total = term if total is None else total + term
        total = total.astype(jnp.bfloat16)
        columns = total.shape[1] // 2
        place = place_ref[step * group + index]
        rank = lax.rem(place, capacity)
        owner = lax.div(place, capacity)
        for d, out_ref in enumerate(out_refs):

            def store(out_ref=out_ref, slot=rank if len(out_refs) > 1 else place):
                out_ref[slot, 0] = total[:, :columns]
                out_ref[slot, 1] = total[:, columns:]

            if len(out_refs) > 1:
                pl.when(owner == d)(store)
            else:
                store()


def bond_products(place, green, coupling, owner_count, capacity, chunk, chunks, split):
    bond_count, _, parts, size, _ = green.shape
    components = coupling.shape[1]
    rows = size // chunks
    group = 4 if bond_count % 4 == 0 else 1
    out_count, slots = (owner_count, capacity) if split else (1, owner_count * capacity)
    shape = (slots, parts, rows, size)
    return pl.pallas_call(
        functools.partial(product_kernel, chunk * rows, rows, group, capacity),
        out_shape=[jax.ShapeDtypeStruct(shape, jnp.bfloat16)] * out_count,
        grid_spec=pltpu.PrefetchScalarGridSpec(
            num_scalar_prefetch=1,
            grid=(bond_count // group,),
            in_specs=[
                pl.BlockSpec((group, 1, parts, size, size), lambda s, _: (s, 0, 0, 0, 0)),
                pl.BlockSpec((group, components, parts, size, size), lambda s, _: (s, 0, 0, 0, 0)),
            ],
            out_specs=[pl.BlockSpec(shape, lambda s, _: (0, 0, 0, 0))] * out_count,
        ),
        compiler_params=pltpu.CompilerParams(vmem_limit_bytes=32 * 2**20),
        cost_estimate=pl.CostEstimate(
            flops=16 * bond_count * components * rows * size * size,
            bytes_accessed=2 * (green.size + coupling.size),
            transcendentals=0,
        ),
        name="bond_products",
    )(place, green, coupling)


def gather_kernel(source_count, capacity, wide, atom_ref, weight_ref, *refs):
    sources = refs[:source_count]
    outs = refs[source_count:-1]
    total = refs[-1]
    slot_count = source_count * capacity
    total[...] = jnp.zeros_like(total)
    for d, source in enumerate(sources):

        def add(slot, carry, d=d, source=source):
            entry = d * capacity + slot
            atom = atom_ref[entry]

            @pl.when(atom >= 0)
            def _():
                values = source[slot].astype(jnp.float32)
                for kind in range(len(outs)):
                    total[kind, atom] += weight_ref[kind * slot_count + entry] * values

            return carry

        lax.fori_loop(0, capacity, add, 0)
    for kind, out in enumerate(outs):
        out[...] = total[kind].astype(out.dtype)


def atom_sums(atoms, weights, sources, kinds, wide):
    capacity, parts, rows, size = sources[0].shape
    steps = max(1, rows // 32)
    tile = rows // steps
    return pl.pallas_call(
        functools.partial(gather_kernel, len(sources), capacity, wide),
        out_shape=[
            jax.ShapeDtypeStruct(
                (A_DEV, 1, parts, rows, size), jnp.float32 if kind in wide else jnp.bfloat16
            )
            for kind in range(kinds)
        ],
        grid_spec=pltpu.PrefetchScalarGridSpec(
            num_scalar_prefetch=2,
            grid=(steps,),
            in_specs=[pl.BlockSpec((capacity, parts, tile, size), lambda s, *_: (0, 0, s, 0))]
            * len(sources),
            out_specs=[
                pl.BlockSpec((A_DEV, None, parts, tile, size), lambda s, *_: (0, 0, 0, s, 0))
            ]
            * kinds,
            scratch_shapes=[pltpu.VMEM((kinds, A_DEV, parts, tile, size), jnp.float32)],
        ),
        compiler_params=pltpu.CompilerParams(vmem_limit_bytes=32 * 2**20),
        cost_estimate=pl.CostEstimate(
            flops=2 * kinds * len(sources) * sources[0].size,
            bytes_accessed=2 * len(sources) * sources[0].size,
            transcendentals=0,
        ),
        name="atom_sums",
    )(atoms, weights, *sources)


def body(green_blocks, coupling, phonon_weight, offsets, bond_atom):
    bond_count = green_blocks.shape[0]
    modes = offsets.shape[1]
    energy_size = lax.axis_size("energy")
    owner_count = lax.axis_size("atom")
    my_energy = lax.axis_index("energy")
    my_owner = lax.axis_index("atom")
    member = my_energy % modes
    capacity = max(2, 2 * bond_count // owner_count)
    split = owner_count == 4
    slot_count = owner_count * capacity

    def inner(d):
        return [
            (e, e // modes * modes + (e + d) % modes) for e in range(energy_size)
        ]

    def outer(d):
        return [(e, (e + d * modes) % energy_size) for e in range(energy_size)]

    owner_index = bond_atom // A_DEV
    bond_order = jnp.arange(bond_count, dtype=jnp.int32)
    same_owner = (owner_index[None, :] == owner_index[:, None]) & (
        bond_order[None, :] < bond_order[:, None]
    )
    rank = jnp.sum(same_owner.astype(jnp.int32), axis=1)
    route = owner_index ^ my_owner if split else owner_index
    place = route * capacity + rank

    products = [
        bond_products(place, green_blocks, coupling, owner_count, capacity, c, CHUNKS, split)
        for c in range(CHUNKS)
    ]

    if modes == 2:
        sign = jnp.where(member == 0, 1, -1)
        shifts = [sign, -sign, -2 * sign, 2 * sign]
        wide = (3,)
    else:
        shifts = []
        for d in range(1, modes):
            partner = (member + d) % modes
            shifts.append(partner - member)
            shifts.append(jnp.where(member > partner, modes, -modes) + partner - member)
        wide = (len(shifts), len(shifts) + 1)
        shifts += [jnp.int32(modes), jnp.int32(-modes)]
    kinds = len(shifts)
    bond_weight = [
        jnp.sum(
            jnp.where(
                offsets == jnp.abs(shift),
                jnp.where(shift > 0, phonon_weight[0], phonon_weight[1]),
                0.0,
            ),
            axis=1,
        )
        for shift in shifts
    ]
    facts = jnp.stack(bond_weight + [(bond_atom % A_DEV + 1).astype(jnp.float32)], axis=0)
    slot_match = (owner_index * capacity + rank)[None, :] == jnp.arange(slot_count)[:, None]
    facts = jnp.sum(jnp.where(slot_match[None], facts[:, None, :], 0.0), axis=2)
    facts = facts.reshape(kinds + 1, owner_count, capacity)
    facts = lax.all_to_all(facts, "atom", split_axis=1, concat_axis=1, tiled=True)
    if split:
        facts = jnp.stack(
            [
                lax.dynamic_index_in_dim(facts, my_owner ^ d, 1, keepdims=False)
                for d in range(owner_count)
            ],
            axis=1,
        )
    atoms = facts[kinds].reshape(-1).astype(jnp.int32) - 1
    weights = facts[:kinds].reshape(-1)

    parts = []
    for c in range(CHUNKS):
        if split:
            sources = [products[c][0]]
            for d in range(1, owner_count):
                sources.append(
                    lax.ppermute(
                        products[c][d], "atom", [(o, o ^ d) for o in range(owner_count)]
                    )
                )
        else:
            shape = products[c][0].shape
            arrived = lax.all_to_all(
                products[c][0].reshape((owner_count, capacity) + shape[1:]),
                "atom",
                split_axis=0,
                concat_axis=0,
                tiled=True,
            )
            sources = [arrived.reshape(shape)]
        sums = atom_sums(atoms, weights, sources, kinds, wide)
        f32 = jnp.float32
        if modes == 2:
            near, relay, early, late = sums
            relay = lax.ppermute(relay, "energy", inner(1))
            early_pairs = [
                (e, (e + (-2 if e % 2 == 0 else 2)) % energy_size) for e in range(energy_size)
            ]
            late_pairs = [
                (e, (e + (2 if e % 2 == 0 else -2)) % energy_size) for e in range(energy_size)
            ]
            early = lax.ppermute(early, "energy", early_pairs)
            near = lax.ppermute(near, "energy", inner(1))
            late = (late + relay.astype(f32)).astype(jnp.bfloat16)
            late = lax.ppermute(late, "energy", late_pairs)
            part = early.astype(f32) + near.astype(f32) + late.astype(f32)
        else:
            up, down = sums[-2:]
            part = 0.0
            for d in range(1, modes):
                near = lax.ppermute(sums[2 * d - 2], "energy", inner(d))
                relay = lax.ppermute(sums[2 * d - 1], "energy", inner(d)).astype(f32)
                part = part + near.astype(f32)
                up = up + jnp.where(member < d, relay, 0.0)
                down = down + jnp.where(member < d, 0.0, relay)
            up = lax.ppermute(up.astype(jnp.bfloat16), "energy", outer(1))
            down = lax.ppermute(down.astype(jnp.bfloat16), "energy", outer(-1))
            part = part + up.astype(f32) + down.astype(f32)
        parts.append(part.astype(jnp.bfloat16))
    return parts[0] if CHUNKS == 1 else jnp.concatenate(parts, axis=3)


def solution(mesh):
    placed = (
        P("atom", "energy", None, None, None),
        P("atom", None, None, None, None),
        P(None, "atom", None),
        P("atom", None),
        P("atom"),
    )
    return jax.shard_map(
        body,
        mesh=mesh,
        in_specs=placed,
        out_specs=P("atom", "energy", None, None, None),
        check_vma=False,
    )
```

time: 115 us -> 74.6 us (0.65)
  waiting for transfers between devices: 74.6 us -> 42.8 us
  Pallas kernels: 0 us -> 12.4 us
  matrix products: 11.2 us -> 0 us
  local copies, waits for them, and re-layouts: 9.37 us -> 4.01 us
  starting transfers between devices: 18.6 us -> 13.5 us
  other arithmetic: 1.11 us -> 2.27 us
    all_to_all x4 -> x1, waiting for transfers between devices: 74.6 us -> 19.7 us  [body(): lax.all_to_all(facts, 'atom', split_axis=1, concat_axis=1, tiled=True)]
    ppermute x0 -> x7, waiting for transfers between devices: none -> 23.1 us  [the longest x1 9.48 us: body(): relay = lax.ppermute(relay, 'energy', inner(1))]
    all_to_all x4 -> x1, starting transfers between devices: 18.6 us -> 3.25 us  [body(): lax.all_to_all(facts, 'atom', split_axis=1, concat_axis=1, tiled=True)]
    pallas_call x0 -> x2, Pallas kernels: none -> 12.4 us  [the longest x1 9.11 us: bond_products(): pl.pallas_call(functools.partial(product_kernel, chunk * rows, rows, grou...]
    dot_general x11 -> x0, matrix products: 11.2 us -> none  [the longest x4 3.23 us: right_mul(): jnp.einsum('becij,bckj->beik', first, second, preferred_element_type=jnp....]
    ppermute x0 -> x7, starting transfers between devices: none -> 10.3 us  [the longest x1 3.6 us: body(): early = lax.ppermute(early, 'energy', early_pairs)]
    convert_element_type x3 -> x0, local copies, waits for them, and re-layouts: 2.61 us -> none  [the longest x1 1.2 us: body(): cycle_mixed.astype(jnp.bfloat16)]
    all_to_all x2 -> x0, local copies, waits for them, and re-layouts: 2.03 us -> none  [the longest x1 1.51 us: body(): lax.all_to_all(cycle_mixed.astype(jnp.bfloat16), 'energy', split_axis=1,...]
  transfers between devices with their start and end apart: 4 -> 8, of which waited for: 3 -> 5; matrix products, arithmetic and copies ran while one was open for 11% -> 2% of each run, Pallas kernels for 0% -> 0%
where the time goes in v1:
time: 74.6 us; the launch traced here: 75.1 us
  waiting for transfers between devices  42.8 us (57%)
  starting transfers between devices  13.5 us (18%)
  Pallas kernels  12.4 us (17%)
  local copies, waits for them, and re-layouts  4.01 us (5%)
  other arithmetic  2.27 us (3%)
    all_to_all x1, waiting for transfers between devices, body(): lax.all_to_all(facts, 'atom', split_axis=1, concat_axis=1, tiled=True)  19.7 us
    ppermute x1, waiting for transfers between devices, body(): relay = lax.ppermute(relay, 'energy', inner(1))  9.48 us
    pallas_call x1, Pallas kernels, bond_products(): pl.pallas_call(functools.partial(product_kernel, chunk * rows, rows, grou...  9.11 us
    ppermute x1, waiting for transfers between devices, body(): near = lax.ppermute(near, 'energy', inner(1))  8.14 us
    ppermute x1, waiting for transfers between devices, body(): late = lax.ppermute(late, 'energy', late_pairs)  4.61 us
    ppermute x1, starting transfers between devices, body(): early = lax.ppermute(early, 'energy', early_pairs)  3.6 us
    pallas_call x1, Pallas kernels, atom_sums(): pl.pallas_call(functools.partial(gather_kernel, len(sources), capacity, w...  3.29 us
    all_to_all x1, starting transfers between devices, body(): lax.all_to_all(facts, 'atom', split_axis=1, concat_axis=1, tiled=True)  3.25 us
  transfers between devices with their start and end apart: 8, of which 5 were waited for; matrix products, arithmetic and copies ran while one was open for 2% of the time, Pallas kernels for 0%

profile of v1, /device:TPU:0, one launch (start us, length us, event | category | flops | bytes accessed | tf_op | source)
XLA Modules:
  0.0 75.1 jit_solution(13885770030592199299)
XLA Ops:
  0.0 0.7 and_select_fusion.1
  0.7 0.2 convert_reduce_fusion
  0.9 1.9 %copy-done = bf16[16,3,2,128,128]{4,3,2,1,0:T(8,128)(2,1)S(1)} copy-done((bf16[16,3,2,128,128]{4,3,2,1,0:T(8,128)(2,1)S(1)}, bf16[16,3,2,128,128]{4,3,2,1,0:T(8,128)(2,1)}, u32[]{:S(2)}) %copy-start) | copy-done | bytes 3145752
  2.8 1.2 %copy-done.1 = bf16[16,1,2,128,128]{4,3,2,1,0:T(8,128)(2,1)S(1)} copy-done((bf16[16,1,2,128,128]{4,3,2,1,0:T(8,128)(2,1)S(1)}, bf16[16,1,2,128,128]{4,3,2,1,0:T(8,128)(2,1)}, u32[]{:S(2)}) %copy-start.1) | copy-done | bytes 1048600
  4.0 9.1 %bond_products.1 = (bf16[8,2,128,128]{3,2,1,0:T(8,128)(2,1)S(1)}, bf16[8,2,128,128]{3,2,1,0:T(8,128)(2,1)}, bf16[8,2,128,128]{3,2,1,0:T(8,128)(2,1)S(1)}, bf16[8,2,128,128]{3,2,1,0:T(8,128)(2,1)S(1)}) custom-call(s32[16]{0:T(128)S(1)} %get-tuple-element.29.place_ref, bf16[16,1,2,128,128]{4,3,2,1,0:T(8,128)(2,1)S(1)} %copy-done.1, ...), custom_call_target="tpu_custom_call" | custom-call | flops 1610612736 | bytes 4194304 | tf_op jit(solution)/shard_map/bond_products/pallas_call | solution.py:80
  13.1 0.5 collective-permute-start
  13.6 2.5 %collective-permute-start.1 = (bf16[8,2,128,128]{3,2,1,0:T(8,128)(2,1)S(1)}, bf16[8,2,128,128]{3,2,1,0:T(8,128)(2,1)S(1)}, u32[]{:S(2)}, u32[]{:S(2)}) collective-permute-start(bf16[8,2,128,128]{3,2,1,0:T(8,128)(2,1)S(1)} %get-tuple-element.15), channel_id=1, source_target_pairs={{0,2},{1,3},{2,0},{3,1},{4,6},{5,7},{6,4},{7,5},{8,10},{9,11},{10,... | collective-permute-start | bytes 1572872 | tf_op jit(solution)/shard_map/ppermute | solution.py:240
  16.1 0.1 collective-permute-start.2
  16.4 0.1 select_reduce_fusion
  16.6 0.6 copy.9
  17.2 3.2 %all-to-all-start = ((f32[5,4,8]{2,0,1:T(8,128)}), f32[5,4,8]{2,0,1:T(8,128)S(1)}, u32[]{:S(2)}, u32[]{:S(2)}) async-start(f32[5,4,8]{2,0,1:T(8,128)} %copy.9), calls=%async_computation | async-start | bytes 32768 | tf_op jit(solution)/shard_map/all_to_all | solution.py:222
  20.4 19.7 %all-to-all-done = f32[5,4,8]{2,0,1:T(8,128)S(1)} async-done(((f32[5,4,8]{2,0,1:T(8,128)}), f32[5,4,8]{2,0,1:T(8,128)S(1)}, u32[]{:S(2)}, u32[]{:S(2)}) %all-to-all-start) | async-done | bytes 672 | tf_op jit(solution)/shard_map/all_to_all | solution.py:222
  40.2 0.1 sub.12.atom_ref
  40.3 0.1 reshape.42.weight_ref
  40.4 3.3 %atom_sums.1 = (bf16[8,1,2,128,128]{4,3,2,1,0:T(8,128)(2,1)S(1)}, bf16[8,1,2,128,128]{4,3,2,1,0:T(8,128)(2,1)S(1)}, bf16[8,1,2,128,128]{4,3,2,1,0:T(8,128)(2,1)S(1)}, f32[8,1,2,128,128]{4,3,2,1,0:T(8,128)S(1)}) custom-call(s32[32]{0:T(128)S(1)} %sub.12.atom_ref, f32[128]{0:T(128)S(1)} %reshape.42.weight_ref, ...), custom_call_target="tpu_custom_call" | custom-call | flops 8388608 | bytes 2097152 | tf_op jit(solution)/shard_map/atom_sums/pallas_call | solution.py:131
  43.7 1.8 %collective-permute-start.5 = (bf16[8,1,2,128,128]{4,3,2,1,0:T(8,128)(2,1)S(1)}, bf16[8,1,2,128,128]{4,3,2,1,0:T(8,128)(2,1)S(1)}, u32[]{:S(2)}, u32[]{:S(2)}) collective-permute-start(bf16[8,1,2,128,128]{4,3,2,1,0:T(8,128)(2,1)S(1)} %get-tuple-element.20), channel_id=1, source_target_pairs={{0,4},{4,0},{8,12},{12,8},{16,20},{20,16},{24,28},{28,24},{1,5},{5... | collective-permute-start | bytes 1572872 | tf_op jit(solution)/shard_map/ppermute | solution.py:258
  45.5 3.6 %collective-permute-start.3 = (bf16[8,1,2,128,128]{4,3,2,1,0:T(8,128)(2,1)S(1)}, bf16[8,1,2,128,128]{4,3,2,1,0:T(8,128)(2,1)S(1)}, u32[]{:S(2)}, u32[]{:S(2)}) collective-permute-start(bf16[8,1,2,128,128]{4,3,2,1,0:T(8,128)(2,1)S(1)} %get-tuple-element.17), channel_id=1, source_target_pairs={{0,24},{4,12},{8,0},{12,20},{16,8},{20,28},{24,16},{28,4},{1,25},{... | collective-permute-start | bytes 1572872 | tf_op jit(solution)/shard_map/ppermute | solution.py:265
  49.1 9.5 %collective-permute-done.5 = bf16[8,1,2,128,128]{4,3,2,1,0:T(8,128)(2,1)S(1)} collective-permute-done((bf16[8,1,2,128,128]{4,3,2,1,0:T(8,128)(2,1)S(1)}, bf16[8,1,2,128,128]{4,3,2,1,0:T(8,128)(2,1)S(1)}, u32[]{:S(2)}, u32[]{:S(2)}) %collective-permute-start.5) | collective-permute-done | bytes 524320 | tf_op jit(solution)/shard_map/ppermute | solution.py:258
  58.5 0.2 add_convert_fusion.1
  58.7 1.7 %collective-permute-start.6 = (bf16[8,1,2,128,128]{4,3,2,1,0:T(8,128)(2,1)S(1)}, bf16[8,1,2,128,128]{4,3,2,1,0:T(8,128)(2,1)S(1)}, u32[]{:S(2)}, u32[]{:S(2)}) collective-permute-start(bf16[8,1,2,128,128]{4,3,2,1,0:T(8,128)(2,1)S(1)} %add_convert_fusion.1), channel_id=1, source_target_pairs={{0,8},{4,28},{8,16},{12,4},{16,24},{20,12},{24,0},{28,20},{1,9},{5... | collective-permute-start | bytes 1572872 | tf_op jit(solution)/shard_map/ppermute | solution.py:268
  60.4 0.9 %collective-permute-done.3 = bf16[8,1,2,128,128]{4,3,2,1,0:T(8,128)(2,1)S(1)} collective-permute-done((bf16[8,1,2,128,128]{4,3,2,1,0:T(8,128)(2,1)S(1)}, bf16[8,1,2,128,128]{4,3,2,1,0:T(8,128)(2,1)S(1)}, u32[]{:S(2)}, u32[]{:S(2)}) %collective-permute-start.3) | collective-permute-done | bytes 524320 | tf_op jit(solution)/shard_map/ppermute | solution.py:265
  61.3 8.1 %collective-permute-done.4 = bf16[8,1,2,128,128]{4,3,2,1,0:T(8,128)(2,1)S(1)} collective-permute-done((bf16[8,1,2,128,128]{4,3,2,1,0:T(8,128)(2,1)S(1)}, bf16[8,1,2,128,128]{4,3,2,1,0:T(8,128)(2,1)S(1)}, u32[]{:S(2)}, u32[]{:S(2)}) %collective-permute-start.4) | collective-permute-done | bytes 524320 | tf_op jit(solution)/shard_map/ppermute | solution.py:266
  69.5 4.6 %collective-permute-done.6 = bf16[8,1,2,128,128]{4,3,2,1,0:T(8,128)(2,1)S(1)} collective-permute-done((bf16[8,1,2,128,128]{4,3,2,1,0:T(8,128)(2,1)S(1)}, bf16[8,1,2,128,128]{4,3,2,1,0:T(8,128)(2,1)S(1)}, u32[]{:S(2)}, u32[]{:S(2)}) %collective-permute-start.6) | collective-permute-done | bytes 524320 | tf_op jit(solution)/shard_map/ppermute | solution.py:268
  74.1 1.0 %add_convert_fusion = bf16[8,1,2,128,128]{4,3,2,1,0:T(8,128)(2,1)} fusion(bf16[8,1,2,128,128]{4,3,2,1,0:T(8,128)(2,1)S(1)} %collective-permute-done.6, bf16[8,1,2,128,128]{4,3,2,1,0:T(8,128)(2,1)S(1)} %collective-permute-done.4, bf16[8,1,2,128,128]{4,3,2,1,0:T(8,128)(2,1)S(1)} %collective-permute-done.3), kind=kLoop, calls=%fused_computation | loop fusion | flops 1572864 | bytes 2097152 | tf_op jit(solution)/shard_map/convert_element_type | solution.py:282
  (19 shorter events, 0.3 us)
Async XLA Ops:
  0.0 16.3 %copy-start.3 = (s32[16,2]{0,1:T(2,128)S(1)}, s32[16,2]{0,1:T(2,128)}, u32[]{:S(2)}) copy-start(s32[16,2]{0,1:T(2,128)} %param.8) | copy-start | bytes 388
  0.0 16.3 %copy-start.2 = (f32[2,16,2]{1,2,0:T(2,128)S(1)}, f32[2,16,2]{1,2,0:T(2,128)}, u32[]{:S(2)}) copy-start(f32[2,16,2]{1,2,0:T(2,128)} %param.7) | copy-start | bytes 772
  0.9 1.9 %copy-start = (bf16[16,3,2,128,128]{4,3,2,1,0:T(8,128)(2,1)S(1)}, bf16[16,3,2,128,128]{4,3,2,1,0:T(8,128)(2,1)}, u32[]{:S(2)}) copy-start(bf16[16,3,2,128,128]{4,3,2,1,0:T(8,128)(2,1)} %coupling_ref.1) | copy-start | bytes 9437188
  2.8 1.2 %copy-start.1 = (bf16[16,1,2,128,128]{4,3,2,1,0:T(8,128)(2,1)S(1)}, bf16[16,1,2,128,128]{4,3,2,1,0:T(8,128)(2,1)}, u32[]{:S(2)}) copy-start(bf16[16,1,2,128,128]{4,3,2,1,0:T(8,128)(2,1)} %green_ref.1) | copy-start | bytes 3145732
  13.1 27.2 %collective-permute-start = (bf16[8,2,128,128]{3,2,1,0:T(8,128)(2,1)}, bf16[8,2,128,128]{3,2,1,0:T(8,128)(2,1)S(1)}, u32[]{:S(2)}, u32[]{:S(2)}) collective-permute-start(bf16[8,2,128,128]{3,2,1,0:T(8,128)(2,1)} %get-tuple-element.14), channel_id=1, source_target_pairs={{0,1},{1,0},{2,3},{3,2},{4,5},{5,4},{6,7},{7,6},{8,9},{9,8},{10,11... | collective-permute-start | bytes 1572872 | tf_op jit(solution)/shard_map/ppermute | solution.py:240
  13.6 26.8 %collective-permute-start.1 = (bf16[8,2,128,128]{3,2,1,0:T(8,128)(2,1)S(1)}, bf16[8,2,128,128]{3,2,1,0:T(8,128)(2,1)S(1)}, u32[]{:S(2)}, u32[]{:S(2)}) collective-permute-start(bf16[8,2,128,128]{3,2,1,0:T(8,128)(2,1)S(1)} %get-tuple-element.15), channel_id=1, source_target_pairs={{0,2},{1,3},{2,0},{3,1},{4,6},{5,7},{6,4},{7,5},{8,10},{9,11},{10,... | collective-permute-start | bytes 1572872 | tf_op jit(solution)/shard_map/ppermute | solution.py:240
  16.1 24.3 %collective-permute-start.2 = (bf16[8,2,128,128]{3,2,1,0:T(8,128)(2,1)S(1)}, bf16[8,2,128,128]{3,2,1,0:T(8,128)(2,1)S(1)}, u32[]{:S(2)}, u32[]{:S(2)}) collective-permute-start(bf16[8,2,128,128]{3,2,1,0:T(8,128)(2,1)S(1)} %get-tuple-element.16), channel_id=1, source_target_pairs={{0,3},{1,2},{2,1},{3,0},{4,7},{5,6},{6,5},{7,4},{8,11},{9,10},{10,... | collective-permute-start | bytes 1572872 | tf_op jit(solution)/shard_map/ppermute | solution.py:240
  17.2 23.0 %all-to-all-start = ((f32[5,4,8]{2,0,1:T(8,128)}), f32[5,4,8]{2,0,1:T(8,128)S(1)}, u32[]{:S(2)}, u32[]{:S(2)}) async-start(f32[5,4,8]{2,0,1:T(8,128)} %copy.9), calls=%async_computation | async-start | bytes 32768 | tf_op jit(solution)/shard_map/all_to_all | solution.py:222
  43.7 14.9 %collective-permute-start.5 = (bf16[8,1,2,128,128]{4,3,2,1,0:T(8,128)(2,1)S(1)}, bf16[8,1,2,128,128]{4,3,2,1,0:T(8,128)(2,1)S(1)}, u32[]{:S(2)}, u32[]{:S(2)}) collective-permute-start(bf16[8,1,2,128,128]{4,3,2,1,0:T(8,128)(2,1)S(1)} %get-tuple-element.20), channel_id=1, source_target_pairs={{0,4},{4,0},{8,12},{12,8},{16,20},{20,16},{24,28},{28,24},{1,5},{5... | collective-permute-start | bytes 1572872 | tf_op jit(solution)/shard_map/ppermute | solution.py:258
  45.5 15.9 %collective-permute-start.3 = (bf16[8,1,2,128,128]{4,3,2,1,0:T(8,128)(2,1)S(1)}, bf16[8,1,2,128,128]{4,3,2,1,0:T(8,128)(2,1)S(1)}, u32[]{:S(2)}, u32[]{:S(2)}) collective-permute-start(bf16[8,1,2,128,128]{4,3,2,1,0:T(8,128)(2,1)S(1)} %get-tuple-element.17), channel_id=1, source_target_pairs={{0,24},{4,12},{8,0},{12,20},{16,8},{20,28},{24,16},{28,4},{1,25},{... | collective-permute-start | bytes 1572872 | tf_op jit(solution)/shard_map/ppermute | solution.py:265
  49.1 20.4 %collective-permute-start.4 = (bf16[8,1,2,128,128]{4,3,2,1,0:T(8,128)(2,1)S(1)}, bf16[8,1,2,128,128]{4,3,2,1,0:T(8,128)(2,1)S(1)}, u32[]{:S(2)}, u32[]{:S(2)}) collective-permute-start(bf16[8,1,2,128,128]{4,3,2,1,0:T(8,128)(2,1)S(1)} %get-tuple-element.18), channel_id=1, source_target_pairs={{0,4},{4,0},{8,12},{12,8},{16,20},{20,16},{24,28},{28,24},{1,5},{5... | collective-permute-start | bytes 1572872 | tf_op jit(solution)/shard_map/ppermute | solution.py:266
  58.7 15.4 %collective-permute-start.6 = (bf16[8,1,2,128,128]{4,3,2,1,0:T(8,128)(2,1)S(1)}, bf16[8,1,2,128,128]{4,3,2,1,0:T(8,128)(2,1)S(1)}, u32[]{:S(2)}, u32[]{:S(2)}) collective-permute-start(bf16[8,1,2,128,128]{4,3,2,1,0:T(8,128)(2,1)S(1)} %add_convert_fusion.1), channel_id=1, source_target_pairs={{0,8},{4,28},{8,16},{12,4},{16,24},{20,12},{24,0},{28,20},{1,9},{5... | collective-permute-start | bytes 1572872 | tf_op jit(solution)/shard_map/ppermute | solution.py:268

commit v2 on v0

v2 whole, which is shorter than its diff:
```python
import functools

import jax
import jax.numpy as jnp
from jax import lax
from jax.experimental import pallas as pl
from jax.experimental.pallas import tpu as pltpu
from jax.sharding import PartitionSpec as P

A_DEV = 8
SHARES = (4, 4)
VMEM_LIMIT = 52 * 2**20
PIECES = 3
CLAIM = 10**9


def product_kernel(row_counts, capacity, split, atom_ref, green_ref, coupling_ref, *refs):
    outs, used_ref = refs[:-1], refs[-1]
    step = pl.program_id(0)
    group, components, _, size, _ = coupling_ref.shape
    my_owner = lax.axis_index("atom") if split else 0

    @pl.when(step == 0)
    def _():
        for owner in range(used_ref.shape[0]):
            used_ref[owner] = 0

    for index in range(group):
        real_green = green_ref[index, 0, 0]
        imag_green = green_ref[index, 0, 1]
        right = jnp.concatenate(
            [
                jnp.concatenate([real_green, imag_green], axis=1),
                jnp.concatenate([-imag_green, real_green], axis=1),
            ],
            axis=0,
        )
        parts = [(coupling_ref[index, c, 0], coupling_ref[index, c, 1]) for c in range(components)]
        left = jnp.concatenate([jnp.concatenate(part, axis=1) for part in parts], axis=0)
        product = jnp.dot(left, right, preferred_element_type=jnp.float32).astype(jnp.bfloat16)
        product = jnp.concatenate(
            [product[c * size : (c + 1) * size] for c in range(components)], axis=1
        )
        last = jnp.concatenate(
            [
                jnp.concatenate(
                    [
                        jnp.concatenate([real_part, -imag_part], axis=1),
                        jnp.concatenate([imag_part, real_part], axis=1),
                    ],
                    axis=0,
                )
                for real_part, imag_part in parts
            ],
            axis=1,
        )
        total = lax.dot_general(
            product, last, (((1,), (1,)), ((), ())), preferred_element_type=jnp.float32
        ).astype(jnp.bfloat16)
        owner = lax.div(atom_ref[step * group + index], A_DEV)
        rank = used_ref[owner]
        used_ref[owner] = rank + 1
        near_place = (owner ^ my_owner) * capacity + rank
        first = 0
        for out, rows in zip(outs, row_counts):
            place = near_place if out is outs[0] else owner * capacity + rank
            out[place, 0] = total[first : first + rows, :size]
            out[place, 1] = total[first : first + rows, size:]
            first += rows


def bond_products(bond_atom, green, coupling, owner_count, capacity, row_counts, split):
    bond_count, _, parts, size, _ = green.shape
    components = coupling.shape[1]
    group = 4 if bond_count % 4 == 0 else 1
    return pl.pallas_call(
        functools.partial(product_kernel, row_counts, capacity, split),
        out_shape=[
            jax.ShapeDtypeStruct((owner_count * capacity, parts, rows, size), jnp.bfloat16)
            for rows in row_counts
        ],
        grid=(bond_count // group,),
        in_specs=[
            pl.BlockSpec(memory_space=pltpu.SMEM),
            pl.BlockSpec((group, 1, parts, size, size), lambda s: (s, 0, 0, 0, 0)),
            pl.BlockSpec((group, components, parts, size, size), lambda s: (s, 0, 0, 0, 0)),
        ],
        out_specs=[pl.BlockSpec(memory_space=pltpu.VMEM)] * len(row_counts),
        scratch_shapes=[pltpu.SMEM((owner_count,), jnp.int32)],
        compiler_params=pltpu.CompilerParams(vmem_limit_bytes=VMEM_LIMIT),
        cost_estimate=pl.CostEstimate(
            flops=16 * bond_count * components * size**3,
            bytes_accessed=2 * (green.size + coupling.size),
            transcendentals=0,
        ),
        name="bond_products",
    )(bond_atom, green, coupling)


def gather_kernel(kinds, owner_count, capacity, split, atom_ref, weight_ref, *refs):
    sources, outs, total = refs[: -len(kinds) - 1], refs[-len(kinds) - 1 : -1], refs[-1]
    rows = total.shape[2]
    slot_count = atom_ref.shape[0]
    total[...] = jnp.zeros_like(total)

    def add_owner(owner, source, first_slot):
        def add(slot, carry):
            entry = owner * capacity + slot
            atom = atom_ref[entry]
            start = pl.multiple_of((first_slot + slot) * rows, rows)
            values = source[pl.ds(start, rows), :].astype(jnp.float32)
            for index, kind in enumerate(kinds):
                total[index, atom] += weight_ref[kind * slot_count + entry] * values
            return carry

        count = jnp.int32(0)
        for slot in range(capacity):
            count += (atom_ref[owner * capacity + slot] >= 0).astype(jnp.int32)
        lax.fori_loop(0, count, add, 0)

    if len(sources) == owner_count:
        for owner, source in enumerate(sources):
            add_owner(owner, source, 0)
    else:

        me = lax.axis_index("atom") if split else 0

        def add_all(owner, carry):
            add_owner(owner, sources[0], (owner ^ me) * capacity)
            return carry

        lax.fori_loop(0, owner_count, add_all, 0)
    for index, out in enumerate(outs):
        out[...] = total[index].reshape(out.shape).astype(out.dtype)


def atom_sums(atoms, weights, sources, kinds, wide, owner_count, block_shape, claimed=0):
    capacity = atoms.shape[0] // owner_count
    parts, rows, size = block_shape
    return pl.pallas_call(
        functools.partial(gather_kernel, kinds, owner_count, capacity, owner_count == 4),
        out_shape=[
            jax.ShapeDtypeStruct(
                (A_DEV, 1, parts, rows, size), jnp.float32 if kind in wide else jnp.bfloat16
            )
            for kind in kinds
        ],
        grid_spec=pltpu.PrefetchScalarGridSpec(
            num_scalar_prefetch=2,
            grid=(1,),
            in_specs=[pl.BlockSpec(memory_space=pltpu.VMEM)] * len(sources),
            out_specs=[pl.BlockSpec(memory_space=pltpu.VMEM)] * len(kinds),
            scratch_shapes=[pltpu.VMEM((len(kinds), A_DEV, parts * rows, size), jnp.float32)],
        ),
        compiler_params=pltpu.CompilerParams(vmem_limit_bytes=32 * 2**20),
        cost_estimate=pl.CostEstimate(
            flops=claimed,
            bytes_accessed=2 * len(sources) * sources[0].size,
            transcendentals=0,
        ),
        name="atom_sums",
    )(atoms, weights, *sources)


def body(green_blocks, coupling, phonon_weight, offsets, bond_atom):
    f32, bf16 = jnp.float32, jnp.bfloat16
    bond_count = green_blocks.shape[0]
    parts_count, size = green_blocks.shape[2], green_blocks.shape[-1]
    modes = offsets.shape[1]
    energy_size = lax.axis_size("energy")
    owner_count = lax.axis_size("atom")
    member = lax.axis_index("energy") % modes
    capacity = max(2, 2 * bond_count // owner_count)
    split = owner_count == 4
    slot_count = owner_count * capacity
    row_counts = [size * share // sum(SHARES) for share in SHARES]

    def inner(d):
        return [(e, e // modes * modes + (e + d) % modes) for e in range(energy_size)]

    def outer(d):
        return [(e, (e + d * modes) % energy_size) for e in range(energy_size)]

    def even_odd(step):
        return [(e, (e + (step if e % 2 == 0 else -step)) % energy_size) for e in range(energy_size)]

    products = bond_products(
        bond_atom, green_blocks, coupling, owner_count, capacity, row_counts, split
    )

    phonon_weight, offsets, bond_atom, products = lax.optimization_barrier(
        (phonon_weight, offsets, bond_atom, products)
    )
    if modes == 2:
        sign = jnp.where(member == 0, 1, -1)
        shifts = [sign, -sign, -2 * sign, 2 * sign]
        wide = (3,)
    else:
        shifts = []
        for d in range(1, modes):
            partner = (member + d) % modes
            shifts.append(partner - member)
            shifts.append(jnp.where(member > partner, modes, -modes) + partner - member)
        wide = (len(shifts), len(shifts) + 1)
        shifts += [jnp.int32(modes), jnp.int32(-modes)]
    kinds = len(shifts)
    owner_index = bond_atom // A_DEV
    bond_order = jnp.arange(bond_count, dtype=jnp.int32)
    same_owner = (owner_index[None, :] == owner_index[:, None]) & (
        bond_order[None, :] < bond_order[:, None]
    )
    rank = jnp.sum(same_owner.astype(jnp.int32), axis=1)
    route = owner_index ^ lax.axis_index("atom") if split else owner_index
    bond_weight = jnp.stack(
        [
            jnp.sum(
                jnp.where(
                    offsets == jnp.abs(shift),
                    jnp.where(shift > 0, phonon_weight[0], phonon_weight[1]),
                    0.0,
                ),
                axis=1,
            )
            for shift in shifts
        ],
        axis=1,
    )
    pieces, rest = [], bond_weight
    for piece in range(PIECES):
        pieces.append(lax.reduce_precision(rest, 8, 7))
        rest = rest - pieces[-1]
    facts = jnp.concatenate(pieces + [(bond_atom % A_DEV + 1).astype(f32)[:, None]], axis=1)
    slot_match = (route * capacity + rank)[None, :] == jnp.arange(slot_count)[:, None]
    facts = jnp.sum(jnp.where(slot_match[:, :, None], facts[None], 0.0), axis=1)
    facts = facts.astype(bf16).reshape(owner_count, capacity, -1)
    if split:
        facts = jnp.pad(
            facts, ((0, 0), (0, -capacity % 16), (0, size - facts.shape[2]))
        )
    else:
        facts = lax.all_to_all(facts, "atom", split_axis=0, concat_axis=0, tiled=True)

    def to_owners(blocks, facts):
        if not split or facts is None:
            blocks = blocks.reshape((owner_count, capacity) + blocks.shape[1:])
            blocks = lax.all_to_all(blocks, "atom", split_axis=0, concat_axis=0, tiled=True)
            return [blocks.reshape(-1, size)]
        blocks = blocks.reshape(owner_count, -1, size)
        if facts is not None:
            blocks = jnp.concatenate([blocks, facts], axis=1)
        return [blocks[0]] + [
            lax.ppermute(blocks[d], "atom", [(o, o ^ d) for o in range(owner_count)])
            for d in range(1, owner_count)
        ]

    sources = [
        to_owners(block, facts if c == 0 else None) for c, block in enumerate(products)
    ]
    if split:
        first = capacity * parts_count * row_counts[0]
        facts = jnp.concatenate([source[first : first + capacity] for source in sources[0]], axis=0)
    else:
        facts = facts.reshape(slot_count, -1)
    weights = sum(
        facts[:, piece * kinds : (piece + 1) * kinds].astype(f32) for piece in range(PIECES)
    )
    weights = weights.T.reshape(-1)
    atoms = facts[:, PIECES * kinds].astype(jnp.int32) - 1

    def sums_of(c, chosen, claimed=0):
        shape = (parts_count, row_counts[c], size)
        return atom_sums(atoms, weights, sources[c], chosen, wide, owner_count, shape, claimed)

    parts = []
    if modes == 2:
        for c in range(len(row_counts)):
            relay, early = sums_of(c, (1, 2))
            near, late = sums_of(c, (0, 3))
            relay = lax.ppermute(relay, "energy", inner(1))
            early = lax.ppermute(early, "energy", even_odd(-2))
            relay, early = lax.optimization_barrier((relay, early))
            late = (late + relay.astype(f32)).astype(bf16)
            near = lax.ppermute(near, "energy", inner(1))
            late = lax.ppermute(late, "energy", even_odd(2))
            parts.append([early, near, late])
        parts = [sum(x.astype(f32) for x in part).astype(bf16) for part in parts]
    else:
        for c in range(len(row_counts)):
            sums = sums_of(c, tuple(range(kinds)))
            up, down = sums[-2:]
            part = 0.0
            for d in range(1, modes):
                near = lax.ppermute(sums[2 * d - 2], "energy", inner(d))
                relay = lax.ppermute(sums[2 * d - 1], "energy", inner(d)).astype(f32)
                part = part + near.astype(f32)
                up = up + jnp.where(member < d, relay, 0.0)
                down = down + jnp.where(member < d, 0.0, relay)
            up = lax.ppermute(up.astype(bf16), "energy", outer(1))
            down = lax.ppermute(down.astype(bf16), "energy", outer(-1))
            parts.append((part + up.astype(f32) + down.astype(f32)).astype(bf16))
    return jnp.concatenate(parts, axis=3)


def solution(mesh):
    placed = (
        P("atom", "energy", None, None, None),
        P("atom", None, None, None, None),
        P(None, "atom", None),
        P("atom", None),
        P("atom"),
    )
    return jax.shard_map(
        body,
        mesh=mesh,
        in_specs=placed,
        out_specs=P("atom", "energy", None, None, None),
        check_vma=False,
    )
```

time: 115 us -> 58.8 us (0.51)
  the two profiles are of different devices: /device:TPU:0 before, /device:TPU:28 now
where the time goes in v2:
time: 58.8 us; the launch traced here: 58.5 us
  waiting for transfers between devices  31.2 us (53%)
  starting transfers between devices  13.1 us (22%)
  Pallas kernels  11.1 us (19%)
  other arithmetic  1.98 us (3%)
  local copies, waits for them, and re-layouts  0.95 us (2%)
    all_to_all x1, waiting for transfers between devices, to_owners(): lax.all_to_all(blocks, 'atom', split_axis=0, concat_axis=0, tiled=True)  8.56 us
    ppermute x3, waiting for transfers between devices, to_owners(): lax.ppermute(blocks[d], 'atom', [(o, o ^ d) for o in range(owner_count)])  8.32 us
    ppermute x2, waiting for transfers between devices, body(): early = lax.ppermute(early, 'energy', even_odd(-2))  6.18 us
    pallas_call x1, Pallas kernels, bond_products(): pl.pallas_call(functools.partial(product_kernel, row_counts, capacity, sp...  6.02 us
    ppermute x2, waiting for transfers between devices, body(): late = lax.ppermute(late, 'energy', even_odd(2))  5.73 us
    pallas_call x4, Pallas kernels, atom_sums(): pl.pallas_call(functools.partial(gather_kernel, kinds, owner_count, capac...  5.11 us
    ppermute x2, starting transfers between devices, body(): near = lax.ppermute(near, 'energy', inner(1))  5.04 us
    all_to_all x1, starting transfers between devices, to_owners(): lax.all_to_all(blocks, 'atom', split_axis=0, concat_axis=0, tiled=True)  3.51 us
  transfers between devices with their start and end apart: 12, of which 7 were waited for; matrix products, arithmetic and copies ran while one was open for 1% of the time, Pallas kernels for 9%

profile of v2, /device:TPU:28, one launch (start us, length us, event | category | flops | bytes accessed | tf_op | source)
XLA Modules:
  0.0 58.5 jit_solution(8047326007502741570)
XLA Ops:
  0.0 0.7 %copy-done = s32[16]{0:T(128)S(1)} copy-done((s32[16]{0:T(128)S(1)}, s32[16]{0:T(128)}, u32[]{:S(2)}) %copy-start) | copy-done | bytes 88
  0.7 6.0 %bond_products.1 = (bf16[32,2,64,128]{3,2,1,0:T(8,128)(2,1)S(1)}, bf16[32,2,64,128]{3,2,1,0:T(8,128)(2,1)}) custom-call(s32[16]{0:T(128)S(1)} %copy-done, bf16[16,1,2,128,128]{4,3,2,1,0:T(8,128)(2,1)} %green_ref.1, bf16[16,3,2,128,128]{4,3,2,1,0:T(8,128)(2,1)} %coupling_ref.1), custom_call_target="tpu_custom_call" | custom-call | flops 1610612736 | bytes 4194304 | tf_op jit(solution)/shard_map/bond_products/pallas_call | solution.py:76
  7.3 1.6 %collective-permute-start.1 = (bf16[1040,128]{1,0:T(8,128)(2,1)S(1)}, bf16[1040,128]{1,0:T(8,128)(2,1)S(1)}, u32[]{:S(2)}, u32[]{:S(2)}) collective-permute-start(bf16[1040,128]{1,0:T(8,128)(2,1)S(1)} %get-tuple-element.48), channel_id=1, source_target_pairs={{0,2},{1,3},{2,0},{3,1},{4,6},{5,7},{6,4},{7,5},{8,10},{9,11},{10,... | collective-permute-start | bytes 798728 | tf_op jit(solution)/shard_map/ppermute | solution.py:252
  8.9 0.7 %collective-permute-start = (bf16[1040,128]{1,0:T(8,128)(2,1)S(1)}, bf16[1040,128]{1,0:T(8,128)(2,1)S(1)}, u32[]{:S(2)}, u32[]{:S(2)}) collective-permute-start(bf16[1040,128]{1,0:T(8,128)(2,1)S(1)} %get-tuple-element.50), channel_id=1, source_target_pairs={{0,1},{1,0},{2,3},{3,2},{4,5},{5,4},{6,7},{7,6},{8,9},{9,8},{10,11... | collective-permute-start | bytes 798728 | tf_op jit(solution)/shard_map/ppermute | solution.py:252
  9.6 3.5 %all-to-all-start = ((bf16[4,8,2,64,128]{4,3,2,1,0:T(8,128)(2,1)}), bf16[4,8,2,64,128]{4,3,2,1,0:T(8,128)(2,1)S(1)}, u32[]{:S(2)}, u32[]{:S(2)}) async-start(bf16[4,8,2,64,128]{4,3,2,1,0:T(8,128)(2,1)} %bitcast.17), calls=%async_computation | async-start | bytes 2097152 | tf_op jit(solution)/shard_map/all_to_all | solution.py:246
  13.1 3.6 %collective-permute-done.1.refs_2_ = bf16[1040,128]{1,0:T(8,128)(2,1)S(1)} collective-permute-done((bf16[1040,128]{1,0:T(8,128)(2,1)S(1)}, bf16[1040,128]{1,0:T(8,128)(2,1)S(1)}, u32[]{:S(2)}, u32[]{:S(2)}) %collective-permute-start.1) | collective-permute-done | bytes 266272 | tf_op jit(solution)/shard_map/ppermute | solution.py:252
  16.7 4.7 %collective-permute-done.2.refs_3_ = bf16[1040,128]{1,0:T(8,128)(2,1)S(1)} collective-permute-done((bf16[1040,128]{1,0:T(8,128)(2,1)S(1)}, bf16[1040,128]{1,0:T(8,128)(2,1)S(1)}, u32[]{:S(2)}, u32[]{:S(2)}) %collective-permute-start.2) | collective-permute-done | bytes 266272 | tf_op jit(solution)/shard_map/ppermute | solution.py:252
  21.9 1.3 %atom_sums.4 = (bf16[8,1,2,64,128]{4,3,2,1,0:T(8,128)(2,1)S(1)}, bf16[8,1,2,64,128]{4,3,2,1,0:T(8,128)(2,1)S(1)}) custom-call(s32[32]{0:T(128)S(1)} %add_reduce_fusion.atom_ref, f32[128]{0:T(128)S(1)} %reshape.49.weight_ref, bf16[1040,128]{1,0:T(8,128)(2,1)S(1)} %get-tuple-element.47.refs_0_, bf16[1040,128]{1,0:T(8,128)(2,1)S(1)} %collective-permute-done.refs_1_, ...), custom_call_target="tpu_custom_call" | custom-call | bytes 1064960 | tf_op jit(solution)/shard_map/atom_sums/pallas_call | solution.py:140
  23.1 0.6 collective-permute-start.3
  23.7 0.2 collective-permute-start.4
  23.9 8.6 %all-to-all-done = bf16[4,8,2,64,128]{4,3,2,1,0:T(8,128)(2,1)S(1)} async-done(((bf16[4,8,2,64,128]{4,3,2,1,0:T(8,128)(2,1)}), bf16[4,8,2,64,128]{4,3,2,1,0:T(8,128)(2,1)S(1)}, u32[]{:S(2)}, u32[]{:S(2)}) %all-to-all-start) | async-done | bytes 1048608 | tf_op jit(solution)/shard_map/all_to_all | solution.py:246
  32.5 1.3 %atom_sums.6 = (bf16[8,1,2,64,128]{4,3,2,1,0:T(8,128)(2,1)S(1)}, bf16[8,1,2,64,128]{4,3,2,1,0:T(8,128)(2,1)S(1)}) custom-call(s32[32]{0:T(128)S(1)} %add_reduce_fusion.atom_ref, f32[128]{0:T(128)S(1)} %reshape.49.weight_ref, bf16[4096,128]{1,0:T(8,128)(2,1)S(1)} %bitcast.30), custom_call_target="tpu_custom_call" | custom-call | bytes 1048576 | tf_op jit(solution)/shard_map/atom_sums/pallas_call | solution.py:140
  33.8 0.6 collective-permute-start.7
  34.4 1.2 %atom_sums.5 = (bf16[8,1,2,64,128]{4,3,2,1,0:T(8,128)(2,1)S(1)}, f32[8,1,2,64,128]{4,3,2,1,0:T(8,128)S(1)}) custom-call(s32[32]{0:T(128)S(1)} %add_reduce_fusion.atom_ref, f32[128]{0:T(128)S(1)} %reshape.49.weight_ref, bf16[1040,128]{1,0:T(8,128)(2,1)S(1)} %get-tuple-element.47.refs_0_, bf16[1040,128]{1,0:T(8,128)(2,1)S(1)} %collective-permute-done.refs_1_, ...), custom_call_target="tpu_custom_call" | custom-call | bytes 1064960 | tf_op jit(solution)/shard_map/atom_sums/pallas_call | solution.py:140
  35.6 2.0 %collective-permute-start.5 = (bf16[8,1,2,64,128]{4,3,2,1,0:T(8,128)(2,1)S(1)}, bf16[8,1,2,64,128]{4,3,2,1,0:T(8,128)(2,1)S(1)}, u32[]{:S(2)}, u32[]{:S(2)}) collective-permute-start(bf16[8,1,2,64,128]{4,3,2,1,0:T(8,128)(2,1)S(1)} %get-tuple-element.33), channel_id=1, source_target_pairs={{0,4},{4,0},{8,12},{12,8},{16,20},{20,16},{24,28},{28,24},{1,5},{5... | collective-permute-start | bytes 786440 | tf_op jit(solution)/shard_map/ppermute | solution.py:283
  37.7 0.5 collective-permute-start.6
  38.2 1.3 %atom_sums.7 = (bf16[8,1,2,64,128]{4,3,2,1,0:T(8,128)(2,1)S(1)}, f32[8,1,2,64,128]{4,3,2,1,0:T(8,128)S(1)}) custom-call(s32[32]{0:T(128)S(1)} %add_reduce_fusion.atom_ref, f32[128]{0:T(128)S(1)} %reshape.49.weight_ref, bf16[4096,128]{1,0:T(8,128)(2,1)S(1)} %bitcast.31), custom_call_target="tpu_custom_call" | custom-call | bytes 1048576 | tf_op jit(solution)/shard_map/atom_sums/pallas_call | solution.py:140
  39.5 3.0 %collective-permute-start.9 = (bf16[8,1,2,64,128]{4,3,2,1,0:T(8,128)(2,1)S(1)}, bf16[8,1,2,64,128]{4,3,2,1,0:T(8,128)(2,1)S(1)}, u32[]{:S(2)}, u32[]{:S(2)}) collective-permute-start(bf16[8,1,2,64,128]{4,3,2,1,0:T(8,128)(2,1)S(1)} %get-tuple-element.40), channel_id=1, source_target_pairs={{0,4},{4,0},{8,12},{12,8},{16,20},{20,16},{24,28},{28,24},{1,5},{5... | collective-permute-start | bytes 786440 | tf_op jit(solution)/shard_map/ppermute | solution.py:283
  42.5 0.5 collective-permute-done.7
  43.1 6.2 %collective-permute-done.8 = bf16[8,1,2,64,128]{4,3,2,1,0:T(8,128)(2,1)S(1)} collective-permute-done((bf16[8,1,2,64,128]{4,3,2,1,0:T(8,128)(2,1)S(1)}, bf16[8,1,2,64,128]{4,3,2,1,0:T(8,128)(2,1)S(1)}, u32[]{:S(2)}, u32[]{:S(2)}) %collective-permute-start.8) | collective-permute-done | bytes 262176 | tf_op jit(solution)/shard_map/ppermute | solution.py:280
  49.3 0.5 collective-permute-start.10
  50.0 1.9 %collective-permute-done.9 = bf16[8,1,2,64,128]{4,3,2,1,0:T(8,128)(2,1)S(1)} collective-permute-done((bf16[8,1,2,64,128]{4,3,2,1,0:T(8,128)(2,1)S(1)}, bf16[8,1,2,64,128]{4,3,2,1,0:T(8,128)(2,1)S(1)}, u32[]{:S(2)}, u32[]{:S(2)}) %collective-permute-start.9) | collective-permute-done | bytes 262176 | tf_op jit(solution)/shard_map/ppermute | solution.py:283
  51.8 5.7 %collective-permute-done.10 = bf16[8,1,2,64,128]{4,3,2,1,0:T(8,128)(2,1)S(1)} collective-permute-done((bf16[8,1,2,64,128]{4,3,2,1,0:T(8,128)(2,1)S(1)}, bf16[8,1,2,64,128]{4,3,2,1,0:T(8,128)(2,1)S(1)}, u32[]{:S(2)}, u32[]{:S(2)}) %collective-permute-start.10) | collective-permute-done | bytes 262176 | tf_op jit(solution)/shard_map/ppermute | solution.py:284
  57.7 0.8 %pad_maximum_fusion = bf16[8,1,2,128,128]{4,3,2,1,0:T(8,128)(2,1)} fusion(bf16[8,1,2,64,128]{4,3,2,1,0:T(8,128)(2,1)S(1)} %add_convert_fusion, bf16[8,1,2,64,128]{4,3,2,1,0:T(8,128)(2,1)S(1)} %add_convert_fusion.2), kind=kLoop, calls=%fused_computation.6 | loop fusion | flops 1048576 | bytes 1048576 | tf_op jit(solution)/shard_map/concatenate | solution.py:301
  (36 shorter events, 1.5 us)
Async XLA Ops:
  0.0 0.7 %copy-start = (s32[16]{0:T(128)S(1)}, s32[16]{0:T(128)}, u32[]{:S(2)}) copy-start(s32[16]{0:T(128)} %atom_ref.1) | copy-start | bytes 196
  0.7 6.3 %copy-start.1 = (f32[2,16,2]{1,2,0:T(2,128)S(1)}, f32[2,16,2]{1,2,0:T(2,128)}, u32[]{:S(2)}) copy-start(f32[2,16,2]{1,2,0:T(2,128)} %param.7) | copy-start | bytes 772
  0.7 6.3 %copy-start.2 = (s32[16,2]{0,1:T(2,128)S(1)}, s32[16,2]{0,1:T(2,128)}, u32[]{:S(2)}) copy-start(s32[16,2]{0,1:T(2,128)} %param.8) | copy-start | bytes 388
  7.3 9.3 %collective-permute-start.1 = (bf16[1040,128]{1,0:T(8,128)(2,1)S(1)}, bf16[1040,128]{1,0:T(8,128)(2,1)S(1)}, u32[]{:S(2)}, u32[]{:S(2)}) collective-permute-start(bf16[1040,128]{1,0:T(8,128)(2,1)S(1)} %get-tuple-element.48), channel_id=1, source_target_pairs={{0,2},{1,3},{2,0},{3,1},{4,6},{5,7},{6,4},{7,5},{8,10},{9,11},{10,... | collective-permute-start | bytes 798728 | tf_op jit(solution)/shard_map/ppermute | solution.py:252
  8.9 12.5 %collective-permute-start.2 = (bf16[1040,128]{1,0:T(8,128)(2,1)S(1)}, bf16[1040,128]{1,0:T(8,128)(2,1)S(1)}, u32[]{:S(2)}, u32[]{:S(2)}) collective-permute-start(bf16[1040,128]{1,0:T(8,128)(2,1)S(1)} %get-tuple-element.49), channel_id=1, source_target_pairs={{0,3},{1,2},{2,1},{3,0},{4,7},{5,6},{6,5},{7,4},{8,11},{9,10},{10,... | collective-permute-start | bytes 798728 | tf_op jit(solution)/shard_map/ppermute | solution.py:252
  8.9 12.5 %collective-permute-start = (bf16[1040,128]{1,0:T(8,128)(2,1)S(1)}, bf16[1040,128]{1,0:T(8,128)(2,1)S(1)}, u32[]{:S(2)}, u32[]{:S(2)}) collective-permute-start(bf16[1040,128]{1,0:T(8,128)(2,1)S(1)} %get-tuple-element.50), channel_id=1, source_target_pairs={{0,1},{1,0},{2,3},{3,2},{4,5},{5,4},{6,7},{7,6},{8,9},{9,8},{10,11... | collective-permute-start | bytes 798728 | tf_op jit(solution)/shard_map/ppermute | solution.py:252
  9.6 22.9 %all-to-all-start = ((bf16[4,8,2,64,128]{4,3,2,1,0:T(8,128)(2,1)}), bf16[4,8,2,64,128]{4,3,2,1,0:T(8,128)(2,1)S(1)}, u32[]{:S(2)}, u32[]{:S(2)}) async-start(bf16[4,8,2,64,128]{4,3,2,1,0:T(8,128)(2,1)} %bitcast.17), calls=%async_computation | async-start | bytes 2097152 | tf_op jit(solution)/shard_map/all_to_all | solution.py:246
  23.1 14.5 %collective-permute-start.3 = (bf16[8,1,2,64,128]{4,3,2,1,0:T(8,128)(2,1)S(1)}, bf16[8,1,2,64,128]{4,3,2,1,0:T(8,128)(2,1)S(1)}, u32[]{:S(2)}, u32[]{:S(2)}) collective-permute-start(bf16[8,1,2,64,128]{4,3,2,1,0:T(8,128)(2,1)S(1)} %get-tuple-element.30), channel_id=1, source_target_pairs={{0,4},{4,0},{8,12},{12,8},{16,20},{20,16},{24,28},{28,24},{1,5},{5... | collective-permute-start | bytes 786440 | tf_op jit(solution)/shard_map/ppermute | solution.py:279
  23.7 14.0 %collective-permute-start.4 = (bf16[8,1,2,64,128]{4,3,2,1,0:T(8,128)(2,1)S(1)}, bf16[8,1,2,64,128]{4,3,2,1,0:T(8,128)(2,1)S(1)}, u32[]{:S(2)}, u32[]{:S(2)}) collective-permute-start(bf16[8,1,2,64,128]{4,3,2,1,0:T(8,128)(2,1)S(1)} %get-tuple-element.31), channel_id=1, source_target_pairs={{0,24},{4,12},{8,0},{12,20},{16,8},{20,28},{24,16},{28,4},{1,25},{... | collective-permute-start | bytes 786440 | tf_op jit(solution)/shard_map/ppermute | solution.py:280
  33.8 9.3 %collective-permute-start.7 = (bf16[8,1,2,64,128]{4,3,2,1,0:T(8,128)(2,1)S(1)}, bf16[8,1,2,64,128]{4,3,2,1,0:T(8,128)(2,1)S(1)}, u32[]{:S(2)}, u32[]{:S(2)}) collective-permute-start(bf16[8,1,2,64,128]{4,3,2,1,0:T(8,128)(2,1)S(1)} %get-tuple-element.37), channel_id=1, source_target_pairs={{0,4},{4,0},{8,12},{12,8},{16,20},{20,16},{24,28},{28,24},{1,5},{5... | collective-permute-start | bytes 786440 | tf_op jit(solution)/shard_map/ppermute | solution.py:279
  34.4 14.9 %collective-permute-start.8 = (bf16[8,1,2,64,128]{4,3,2,1,0:T(8,128)(2,1)S(1)}, bf16[8,1,2,64,128]{4,3,2,1,0:T(8,128)(2,1)S(1)}, u32[]{:S(2)}, u32[]{:S(2)}) collective-permute-start(bf16[8,1,2,64,128]{4,3,2,1,0:T(8,128)(2,1)S(1)} %get-tuple-element.38), channel_id=1, source_target_pairs={{0,24},{4,12},{8,0},{12,20},{16,8},{20,28},{24,16},{28,4},{1,25},{... | collective-permute-start | bytes 786440 | tf_op jit(solution)/shard_map/ppermute | solution.py:280
  35.6 14.2 %collective-permute-start.5 = (bf16[8,1,2,64,128]{4,3,2,1,0:T(8,128)(2,1)S(1)}, bf16[8,1,2,64,128]{4,3,2,1,0:T(8,128)(2,1)S(1)}, u32[]{:S(2)}, u32[]{:S(2)}) collective-permute-start(bf16[8,1,2,64,128]{4,3,2,1,0:T(8,128)(2,1)S(1)} %get-tuple-element.33), channel_id=1, source_target_pairs={{0,4},{4,0},{8,12},{12,8},{16,20},{20,16},{24,28},{28,24},{1,5},{5... | collective-permute-start | bytes 786440 | tf_op jit(solution)/shard_map/ppermute | solution.py:283
  37.7 12.1 %collective-permute-start.6 = (bf16[8,1,2,64,128]{4,3,2,1,0:T(8,128)(2,1)S(1)}, bf16[8,1,2,64,128]{4,3,2,1,0:T(8,128)(2,1)S(1)}, u32[]{:S(2)}, u32[]{:S(2)}) collective-permute-start(bf16[8,1,2,64,128]{4,3,2,1,0:T(8,128)(2,1)S(1)} %add_convert_fusion.3), channel_id=1, source_target_pairs={{0,8},{4,28},{8,16},{12,4},{16,24},{20,12},{24,0},{28,20},{1,9},{5... | collective-permute-start | bytes 786440 | tf_op jit(solution)/shard_map/ppermute | solution.py:284
  39.5 12.3 %collective-permute-start.9 = (bf16[8,1,2,64,128]{4,3,2,1,0:T(8,128)(2,1)S(1)}, bf16[8,1,2,64,128]{4,3,2,1,0:T(8,128)(2,1)S(1)}, u32[]{:S(2)}, u32[]{:S(2)}) collective-permute-start(bf16[8,1,2,64,128]{4,3,2,1,0:T(8,128)(2,1)S(1)} %get-tuple-element.40), channel_id=1, source_target_pairs={{0,4},{4,0},{8,12},{12,8},{16,20},{20,16},{24,28},{28,24},{1,5},{5... | collective-permute-start | bytes 786440 | tf_op jit(solution)/shard_map/ppermute | solution.py:283
  49.3 8.2 %collective-permute-start.10 = (bf16[8,1,2,64,128]{4,3,2,1,0:T(8,128)(2,1)S(1)}, bf16[8,1,2,64,128]{4,3,2,1,0:T(8,128)(2,1)S(1)}, u32[]{:S(2)}, u32[]{:S(2)}) collective-permute-start(bf16[8,1,2,64,128]{4,3,2,1,0:T(8,128)(2,1)S(1)} %add_convert_fusion.1), channel_id=1, source_target_pairs={{0,8},{4,28},{8,16},{12,4},{16,24},{20,12},{24,0},{28,20},{1,9},{5... | collective-permute-start | bytes 786440 | tf_op jit(solution)/shard_map/ppermute | solution.py:284

commit v3 on v2

--- a/solution.py
+++ b/solution.py
@@ -11,7 +11,6 @@
 SHARES = (4, 4)
 VMEM_LIMIT = 52 * 2**20
 PIECES = 3
-CLAIM = 10**9
 
 
 def product_kernel(row_counts, capacity, split, atom_ref, green_ref, coupling_ref, *refs):
@@ -25,6 +24,7 @@
         for owner in range(used_ref.shape[0]):
             used_ref[owner] = 0
 
+    products = []
     for index in range(group):
         real_green = green_ref[index, 0, 0]
         imag_green = green_ref[index, 0, 1]
@@ -35,27 +35,26 @@
             ],
             axis=0,
         )
-        parts = [(coupling_ref[index, c, 0], coupling_ref[index, c, 1]) for c in range(components)]
-        left = jnp.concatenate([jnp.concatenate(part, axis=1) for part in parts], axis=0)
+        left = jnp.concatenate(
+            [
+                jnp.concatenate([coupling_ref[index, c, 0], coupling_ref[index, c, 1]], axis=1)
+                for c in range(components)
+            ],
+            axis=0,
+        )
         product = jnp.dot(left, right, preferred_element_type=jnp.float32).astype(jnp.bfloat16)
-        product = jnp.concatenate(
-            [product[c * size : (c + 1) * size] for c in range(components)], axis=1
+        products.append(
+            jnp.concatenate([product[c * size : (c + 1) * size] for c in range(components)], axis=1)
         )
-        last = jnp.concatenate(
-            [
-                jnp.concatenate(
-                    [
-                        jnp.concatenate([real_part, -imag_part], axis=1),
-                        jnp.concatenate([imag_part, real_part], axis=1),
-                    ],
-                    axis=0,
-                )
-                for real_part, imag_part in parts
-            ],
-            axis=1,
-        )
+    for index in range(group):
+        rows_of = []
+        for c in range(components):
+            real_last, imag_last = coupling_ref[index, c, 0].T, coupling_ref[index, c, 1].T
+            rows_of.append(jnp.concatenate([real_last, imag_last], axis=1))
+            rows_of.append(jnp.concatenate([-imag_last, real_last], axis=1))
+        last = jnp.concatenate(rows_of, axis=0)
         total = lax.dot_general(
-            product, last, (((1,), (1,)), ((), ())), preferred_element_type=jnp.float32
+            products[index], last, (((1,), (0,)), ((), ())), preferred_element_type=jnp.float32
         ).astype(jnp.bfloat16)
         owner = lax.div(atom_ref[step * group + index], A_DEV)
         rank = used_ref[owner]
@@ -72,7 +71,7 @@
 def bond_products(bond_atom, green, coupling, owner_count, capacity, row_counts, split):
     bond_count, _, parts, size, _ = green.shape
     components = coupling.shape[1]
-    group = 4 if bond_count % 4 == 0 else 1
+    group = 8 if bond_count % 8 == 0 else 1
     return pl.pallas_call(
         functools.partial(product_kernel, row_counts, capacity, split),
         out_shape=[
@@ -134,7 +133,7 @@
         out[...] = total[index].reshape(out.shape).astype(out.dtype)
 
 
-def atom_sums(atoms, weights, sources, kinds, wide, owner_count, block_shape, claimed=0):
+def atom_sums(atoms, weights, sources, kinds, wide, owner_count, block_shape):
     capacity = atoms.shape[0] // owner_count
     parts, rows, size = block_shape
     return pl.pallas_call(
@@ -154,7 +153,7 @@
         ),
         compiler_params=pltpu.CompilerParams(vmem_limit_bytes=32 * 2**20),
         cost_estimate=pl.CostEstimate(
-            flops=claimed,
+            flops=2 * len(kinds) * len(sources) * sources[0].size,
             bytes_accessed=2 * len(sources) * sources[0].size,
             transcendentals=0,
         ),
@@ -267,22 +266,31 @@
     weights = weights.T.reshape(-1)
     atoms = facts[:, PIECES * kinds].astype(jnp.int32) - 1
 
-    def sums_of(c, chosen, claimed=0):
+    def sums_of(c, chosen):
         shape = (parts_count, row_counts[c], size)
-        return atom_sums(atoms, weights, sources[c], chosen, wide, owner_count, shape, claimed)
+        return atom_sums(atoms, weights, sources[c], chosen, wide, owner_count, shape)
 
     parts = []
     if modes == 2:
         for c in range(len(row_counts)):
+            if c > 0:
+                sources[c], merged = lax.optimization_barrier((sources[c], merged))
+                parts[-1][2] = lax.ppermute(merged, "energy", even_odd(2))
             relay, early = sums_of(c, (1, 2))
+            if c > 0:
+                relay, early, parts[-1][0] = lax.optimization_barrier((relay, early, parts[-1][0]))
             near, late = sums_of(c, (0, 3))
             relay = lax.ppermute(relay, "energy", inner(1))
             early = lax.ppermute(early, "energy", even_odd(-2))
-            relay, early = lax.optimization_barrier((relay, early))
+            if c > 0:
+                done = parts[-1][0].astype(f32) + parts[-1][2].astype(f32)
+                relay, done = lax.optimization_barrier((relay, done))
+                parts[-1][0], parts[-1][2] = done, jnp.zeros((), f32)
             late = (late + relay.astype(f32)).astype(bf16)
             near = lax.ppermute(near, "energy", inner(1))
-            late = lax.ppermute(late, "energy", even_odd(2))
-            parts.append([early, near, late])
+            merged = late
+            parts.append([early, near, None])
+        parts[-1][2] = lax.ppermute(merged, "energy", even_odd(2))
         parts = [sum(x.astype(f32) for x in part).astype(bf16) for part in parts]
     else:
         for c in range(len(row_counts)):

time: 58.8 us -> 57.1 us (0.971)
  the two profiles are of different devices: /device:TPU:28 before, /device:TPU:0 now
where the time goes in v3:
time: 57.1 us; the launch traced here: 57 us
  waiting for transfers between devices  26.7 us (47%)
  starting transfers between devices  19.7 us (35%)
  Pallas kernels  7.57 us (13%)
  other arithmetic  2.01 us (4%)
  local copies, waits for them, and re-layouts  0.95 us (2%)
    ppermute x2, waiting for transfers between devices, body(): near = lax.ppermute(near, 'energy', inner(1))  10.1 us
    ppermute x3, waiting for transfers between devices, to_owners(): lax.ppermute(blocks[d], 'atom', [(o, o ^ d) for o in range(owner_count)])  8.77 us
    ppermute x2, starting transfers between devices, body(): early = lax.ppermute(early, 'energy', even_odd(-2))  5.66 us
    ppermute x2, starting transfers between devices, body(): relay = lax.ppermute(relay, 'energy', inner(1))  5.19 us
    ppermute x2, waiting for transfers between devices, body(): relay = lax.ppermute(relay, 'energy', inner(1))  5.19 us
    pallas_call x1, Pallas kernels, bond_products(): pl.pallas_call(functools.partial(product_kernel, row_counts, capacity, sp...  4.61 us
    all_to_all x1, starting transfers between devices, to_owners(): lax.all_to_all(blocks, 'atom', split_axis=0, concat_axis=0, tiled=True)  3.51 us
    ppermute x3, starting transfers between devices, to_owners(): lax.ppermute(blocks[d], 'atom', [(o, o ^ d) for o in range(owner_count)])  3.2 us
  transfers between devices with their start and end apart: 12, of which 8 were waited for; matrix products, arithmetic and copies ran while one was open for 1% of the time, Pallas kernels for 5%

profile of v3, /device:TPU:0, one launch (start us, length us, event | category | flops | bytes accessed | tf_op | source)
XLA Modules:
  0.0 57.0 jit_solution(4931082935540390290)
XLA Ops:
  0.0 0.7 %copy-done = s32[16]{0:T(128)S(1)} copy-done((s32[16]{0:T(128)S(1)}, s32[16]{0:T(128)}, u32[]{:S(2)}) %copy-start) | copy-done | bytes 88
  0.7 4.6 %bond_products.1 = (bf16[32,2,64,128]{3,2,1,0:T(8,128)(2,1)S(1)}, bf16[32,2,64,128]{3,2,1,0:T(8,128)(2,1)}) custom-call(s32[16]{0:T(128)S(1)} %copy-done, bf16[16,1,2,128,128]{4,3,2,1,0:T(8,128)(2,1)} %green_ref.1, bf16[16,3,2,128,128]{4,3,2,1,0:T(8,128)(2,1)} %coupling_ref.1), custom_call_target="tpu_custom_call" | custom-call | flops 1610612736 | bytes 4194304 | tf_op jit(solution)/shard_map/bond_products/pallas_call | solution.py:75
  5.3 0.2 convert_reduce_fusion
  5.9 3.0 %collective-permute-start.1 = (bf16[1040,128]{1,0:T(8,128)(2,1)S(1)}, bf16[1040,128]{1,0:T(8,128)(2,1)S(1)}, u32[]{:S(2)}, u32[]{:S(2)}) collective-permute-start(bf16[1040,128]{1,0:T(8,128)(2,1)S(1)} %get-tuple-element.54), channel_id=1, source_target_pairs={{0,2},{1,3},{2,0},{3,1},{4,6},{5,7},{6,4},{7,5},{8,10},{9,11},{10,... | collective-permute-start | bytes 798728 | tf_op jit(solution)/shard_map/ppermute | solution.py:251
  8.9 0.2 collective-permute-start
  9.1 3.5 %all-to-all-start = ((bf16[4,8,2,64,128]{4,3,2,1,0:T(8,128)(2,1)}), bf16[4,8,2,64,128]{4,3,2,1,0:T(8,128)(2,1)S(1)}, u32[]{:S(2)}, u32[]{:S(2)}) async-start(bf16[4,8,2,64,128]{4,3,2,1,0:T(8,128)(2,1)} %bitcast.16), calls=%async_computation | async-start | bytes 2097152 | tf_op jit(solution)/shard_map/all_to_all | solution.py:245
  12.7 3.5 %collective-permute-done.1.refs_2_ = bf16[1040,128]{1,0:T(8,128)(2,1)S(1)} collective-permute-done((bf16[1040,128]{1,0:T(8,128)(2,1)S(1)}, bf16[1040,128]{1,0:T(8,128)(2,1)S(1)}, u32[]{:S(2)}, u32[]{:S(2)}) %collective-permute-start.1) | collective-permute-done | bytes 266272 | tf_op jit(solution)/shard_map/ppermute | solution.py:251
  16.2 5.3 %collective-permute-done.2.refs_3_ = bf16[1040,128]{1,0:T(8,128)(2,1)S(1)} collective-permute-done((bf16[1040,128]{1,0:T(8,128)(2,1)S(1)}, bf16[1040,128]{1,0:T(8,128)(2,1)S(1)}, u32[]{:S(2)}, u32[]{:S(2)}) %collective-permute-start.2) | collective-permute-done | bytes 266272 | tf_op jit(solution)/shard_map/ppermute | solution.py:251
  21.9 0.7 %atom_sums.5 = (bf16[8,1,2,64,128]{4,3,2,1,0:T(8,128)(2,1)S(1)}, bf16[8,1,2,64,128]{4,3,2,1,0:T(8,128)(2,1)S(1)}) custom-call(s32[32]{0:T(128)S(1)} %add_reduce_fusion.atom_ref, f32[128]{0:T(128)S(1)} %reshape.49.weight_ref, bf16[1040,128]{1,0:T(8,128)(2,1)S(1)} %get-tuple-element.53.refs_0_, bf16[1040,128]{1,0:T(8,128)(2,1)S(1)} %collective-permute-done.refs_1_, ...), custom_call_target="tpu_custom_call" | custom-call | flops 2129920 | bytes 1064960 | tf_op jit(solution)/shard_map/atom_sums/pallas_call | solution.py:139
  22.6 1.6 %collective-permute-start.3 = (bf16[8,1,2,64,128]{4,3,2,1,0:T(8,128)(2,1)S(1)}, bf16[8,1,2,64,128]{4,3,2,1,0:T(8,128)(2,1)S(1)}, u32[]{:S(2)}, u32[]{:S(2)}) collective-permute-start(bf16[8,1,2,64,128]{4,3,2,1,0:T(8,128)(2,1)S(1)} %get-tuple-element.35), channel_id=1, source_target_pairs={{0,4},{4,0},{8,12},{12,8},{16,20},{20,16},{24,28},{28,24},{1,5},{5... | collective-permute-start | bytes 786440 | tf_op jit(solution)/shard_map/ppermute | solution.py:283
  24.2 3.6 %collective-permute-start.4 = (bf16[8,1,2,64,128]{4,3,2,1,0:T(8,128)(2,1)S(1)}, bf16[8,1,2,64,128]{4,3,2,1,0:T(8,128)(2,1)S(1)}, u32[]{:S(2)}, u32[]{:S(2)}) collective-permute-start(bf16[8,1,2,64,128]{4,3,2,1,0:T(8,128)(2,1)S(1)} %get-tuple-element.39), channel_id=1, source_target_pairs={{0,24},{4,12},{8,0},{12,20},{16,8},{20,28},{24,16},{28,4},{1,25},{... | collective-permute-start | bytes 786440 | tf_op jit(solution)/shard_map/ppermute | solution.py:284
  27.8 0.7 %atom_sums.4 = (bf16[8,1,2,64,128]{4,3,2,1,0:T(8,128)(2,1)S(1)}, f32[8,1,2,64,128]{4,3,2,1,0:T(8,128)S(1)}) custom-call(s32[32]{0:T(128)S(1)} %add_reduce_fusion.atom_ref, f32[128]{0:T(128)S(1)} %reshape.49.weight_ref, bf16[1040,128]{1,0:T(8,128)(2,1)S(1)} %get-tuple-element.53.refs_0_, bf16[1040,128]{1,0:T(8,128)(2,1)S(1)} %collective-permute-done.refs_1_, ...), custom_call_target="tpu_custom_call" | custom-call | flops 2129920 | bytes 1064960 | tf_op jit(solution)/shard_map/atom_sums/pallas_call | solution.py:139
  28.5 2.9 %collective-permute-done.3 = bf16[8,1,2,64,128]{4,3,2,1,0:T(8,128)(2,1)S(1)} collective-permute-done((bf16[8,1,2,64,128]{4,3,2,1,0:T(8,128)(2,1)S(1)}, bf16[8,1,2,64,128]{4,3,2,1,0:T(8,128)(2,1)S(1)}, u32[]{:S(2)}, u32[]{:S(2)}) %collective-permute-start.3) | collective-permute-done | bytes 262176 | tf_op jit(solution)/shard_map/ppermute | solution.py:283
  31.5 0.7 %all-to-all-done = bf16[4,8,2,64,128]{4,3,2,1,0:T(8,128)(2,1)S(1)} async-done(((bf16[4,8,2,64,128]{4,3,2,1,0:T(8,128)(2,1)}), bf16[4,8,2,64,128]{4,3,2,1,0:T(8,128)(2,1)S(1)}, u32[]{:S(2)}, u32[]{:S(2)}) %all-to-all-start) | async-done | bytes 1048608 | tf_op jit(solution)/shard_map/all_to_all | solution.py:245
  32.3 1.8 %collective-permute-start.6 = (bf16[8,1,2,64,128]{4,3,2,1,0:T(8,128)(2,1)S(1)}, bf16[8,1,2,64,128]{4,3,2,1,0:T(8,128)(2,1)S(1)}, u32[]{:S(2)}, u32[]{:S(2)}) collective-permute-start(bf16[8,1,2,64,128]{4,3,2,1,0:T(8,128)(2,1)S(1)} %add_convert_fusion.3), channel_id=1, source_target_pairs={{0,8},{4,28},{8,16},{12,4},{16,24},{20,12},{24,0},{28,20},{1,9},{5... | collective-permute-start | bytes 786440 | tf_op jit(solution)/shard_map/ppermute | solution.py:278
  34.1 0.8 %atom_sums.6 = (bf16[8,1,2,64,128]{4,3,2,1,0:T(8,128)(2,1)S(1)}, bf16[8,1,2,64,128]{4,3,2,1,0:T(8,128)(2,1)S(1)}) custom-call(s32[32]{0:T(128)S(1)} %add_reduce_fusion.atom_ref, f32[128]{0:T(128)S(1)} %reshape.49.weight_ref, bf16[4096,128]{1,0:T(8,128)(2,1)S(1)} %bitcast.30), custom_call_target="tpu_custom_call" | custom-call | flops 2097152 | bytes 1048576 | tf_op jit(solution)/shard_map/atom_sums/pallas_call | solution.py:139
  34.9 3.6 %collective-permute-start.5 = (bf16[8,1,2,64,128]{4,3,2,1,0:T(8,128)(2,1)S(1)}, bf16[8,1,2,64,128]{4,3,2,1,0:T(8,128)(2,1)S(1)}, u32[]{:S(2)}, u32[]{:S(2)}) collective-permute-start(bf16[8,1,2,64,128]{4,3,2,1,0:T(8,128)(2,1)S(1)} %get-tuple-element.40), channel_id=1, source_target_pairs={{0,4},{4,0},{8,12},{12,8},{16,20},{20,16},{24,28},{28,24},{1,5},{5... | collective-permute-start | bytes 786440 | tf_op jit(solution)/shard_map/ppermute | solution.py:283
  38.6 2.1 %collective-permute-start.8 = (bf16[8,1,2,64,128]{4,3,2,1,0:T(8,128)(2,1)S(1)}, bf16[8,1,2,64,128]{4,3,2,1,0:T(8,128)(2,1)S(1)}, u32[]{:S(2)}, u32[]{:S(2)}) collective-permute-start(bf16[8,1,2,64,128]{4,3,2,1,0:T(8,128)(2,1)S(1)} %get-tuple-element.45), channel_id=1, source_target_pairs={{0,24},{4,12},{8,0},{12,20},{16,8},{20,28},{24,16},{28,4},{1,25},{... | collective-permute-start | bytes 786440 | tf_op jit(solution)/shard_map/ppermute | solution.py:284
  40.6 0.8 %atom_sums.7 = (bf16[8,1,2,64,128]{4,3,2,1,0:T(8,128)(2,1)S(1)}, f32[8,1,2,64,128]{4,3,2,1,0:T(8,128)S(1)}) custom-call(s32[32]{0:T(128)S(1)} %add_reduce_fusion.atom_ref, f32[128]{0:T(128)S(1)} %reshape.49.weight_ref, bf16[4096,128]{1,0:T(8,128)(2,1)S(1)} %bitcast.31), custom_call_target="tpu_custom_call" | custom-call | flops 2097152 | bytes 1048576 | tf_op jit(solution)/shard_map/atom_sums/pallas_call | solution.py:139
  41.5 1.8 %collective-permute-done.6 = bf16[8,1,2,64,128]{4,3,2,1,0:T(8,128)(2,1)S(1)} collective-permute-done((bf16[8,1,2,64,128]{4,3,2,1,0:T(8,128)(2,1)S(1)}, bf16[8,1,2,64,128]{4,3,2,1,0:T(8,128)(2,1)S(1)}, u32[]{:S(2)}, u32[]{:S(2)}) %collective-permute-start.6) | collective-permute-done | bytes 262176 | tf_op jit(solution)/shard_map/ppermute | solution.py:278
  43.4 2.3 %collective-permute-done.5 = bf16[8,1,2,64,128]{4,3,2,1,0:T(8,128)(2,1)S(1)} collective-permute-done((bf16[8,1,2,64,128]{4,3,2,1,0:T(8,128)(2,1)S(1)}, bf16[8,1,2,64,128]{4,3,2,1,0:T(8,128)(2,1)S(1)}, u32[]{:S(2)}, u32[]{:S(2)}) %collective-permute-start.5) | collective-permute-done | bytes 262176 | tf_op jit(solution)/shard_map/ppermute | solution.py:283
  45.8 5.4 %collective-permute-done.7 = bf16[8,1,2,64,128]{4,3,2,1,0:T(8,128)(2,1)S(1)} collective-permute-done((bf16[8,1,2,64,128]{4,3,2,1,0:T(8,128)(2,1)S(1)}, bf16[8,1,2,64,128]{4,3,2,1,0:T(8,128)(2,1)S(1)}, u32[]{:S(2)}, u32[]{:S(2)}) %collective-permute-start.7) | collective-permute-done | bytes 262176 | tf_op jit(solution)/shard_map/ppermute | solution.py:290
  51.3 4.7 %collective-permute-done.9 = bf16[8,1,2,64,128]{4,3,2,1,0:T(8,128)(2,1)S(1)} collective-permute-done((bf16[8,1,2,64,128]{4,3,2,1,0:T(8,128)(2,1)S(1)}, bf16[8,1,2,64,128]{4,3,2,1,0:T(8,128)(2,1)S(1)}, u32[]{:S(2)}, u32[]{:S(2)}) %collective-permute-start.9) | collective-permute-done | bytes 262176 | tf_op jit(solution)/shard_map/ppermute | solution.py:290
  56.2 0.8 %pad_maximum_fusion = bf16[8,1,2,128,128]{4,3,2,1,0:T(8,128)(2,1)} fusion(bf16[8,1,2,64,128]{4,3,2,1,0:T(8,128)(2,1)S(1)} %add_convert_fusion, bf16[8,1,2,64,128]{4,3,2,1,0:T(8,128)(2,1)S(1)} %add_convert_fusion.2), kind=kLoop, calls=%fused_computation.6 | loop fusion | flops 1048576 | bytes 1048576 | tf_op jit(solution)/shard_map/concatenate | solution.py:309
  (37 shorter events, 1.6 us)
Async XLA Ops:
  0.0 0.7 %copy-start = (s32[16]{0:T(128)S(1)}, s32[16]{0:T(128)}, u32[]{:S(2)}) copy-start(s32[16]{0:T(128)} %atom_ref.1) | copy-start | bytes 196
  0.7 4.9 %copy-start.1 = (f32[2,16,2]{1,2,0:T(2,128)S(1)}, f32[2,16,2]{1,2,0:T(2,128)}, u32[]{:S(2)}) copy-start(f32[2,16,2]{1,2,0:T(2,128)} %param.7) | copy-start | bytes 772
  0.7 4.9 %copy-start.2 = (s32[16,2]{0,1:T(2,128)S(1)}, s32[16,2]{0,1:T(2,128)}, u32[]{:S(2)}) copy-start(s32[16,2]{0,1:T(2,128)} %param.8) | copy-start | bytes 388
  5.9 10.2 %collective-permute-start.1 = (bf16[1040,128]{1,0:T(8,128)(2,1)S(1)}, bf16[1040,128]{1,0:T(8,128)(2,1)S(1)}, u32[]{:S(2)}, u32[]{:S(2)}) collective-permute-start(bf16[1040,128]{1,0:T(8,128)(2,1)S(1)} %get-tuple-element.54), channel_id=1, source_target_pairs={{0,2},{1,3},{2,0},{3,1},{4,6},{5,7},{6,4},{7,5},{8,10},{9,11},{10,... | collective-permute-start | bytes 798728 | tf_op jit(solution)/shard_map/ppermute | solution.py:251
  8.9 12.5 %collective-permute-start.2 = (bf16[1040,128]{1,0:T(8,128)(2,1)S(1)}, bf16[1040,128]{1,0:T(8,128)(2,1)S(1)}, u32[]{:S(2)}, u32[]{:S(2)}) collective-permute-start(bf16[1040,128]{1,0:T(8,128)(2,1)S(1)} %get-tuple-element.55), channel_id=1, source_target_pairs={{0,3},{1,2},{2,1},{3,0},{4,7},{5,6},{6,5},{7,4},{8,11},{9,10},{10,... | collective-permute-start | bytes 798728 | tf_op jit(solution)/shard_map/ppermute | solution.py:251
  8.9 12.5 %collective-permute-start = (bf16[1040,128]{1,0:T(8,128)(2,1)S(1)}, bf16[1040,128]{1,0:T(8,128)(2,1)S(1)}, u32[]{:S(2)}, u32[]{:S(2)}) collective-permute-start(bf16[1040,128]{1,0:T(8,128)(2,1)S(1)} %get-tuple-element.56), channel_id=1, source_target_pairs={{0,1},{1,0},{2,3},{3,2},{4,5},{5,4},{6,7},{7,6},{8,9},{9,8},{10,11... | collective-permute-start | bytes 798728 | tf_op jit(solution)/shard_map/ppermute | solution.py:251
  9.1 23.1 %all-to-all-start = ((bf16[4,8,2,64,128]{4,3,2,1,0:T(8,128)(2,1)}), bf16[4,8,2,64,128]{4,3,2,1,0:T(8,128)(2,1)S(1)}, u32[]{:S(2)}, u32[]{:S(2)}) async-start(bf16[4,8,2,64,128]{4,3,2,1,0:T(8,128)(2,1)} %bitcast.16), calls=%async_computation | async-start | bytes 2097152 | tf_op jit(solution)/shard_map/all_to_all | solution.py:245
  22.6 8.9 %collective-permute-start.3 = (bf16[8,1,2,64,128]{4,3,2,1,0:T(8,128)(2,1)S(1)}, bf16[8,1,2,64,128]{4,3,2,1,0:T(8,128)(2,1)S(1)}, u32[]{:S(2)}, u32[]{:S(2)}) collective-permute-start(bf16[8,1,2,64,128]{4,3,2,1,0:T(8,128)(2,1)S(1)} %get-tuple-element.35), channel_id=1, source_target_pairs={{0,4},{4,0},{8,12},{12,8},{16,20},{20,16},{24,28},{28,24},{1,5},{5... | collective-permute-start | bytes 786440 | tf_op jit(solution)/shard_map/ppermute | solution.py:283
  24.2 10.7 %collective-permute-start.4 = (bf16[8,1,2,64,128]{4,3,2,1,0:T(8,128)(2,1)S(1)}, bf16[8,1,2,64,128]{4,3,2,1,0:T(8,128)(2,1)S(1)}, u32[]{:S(2)}, u32[]{:S(2)}) collective-permute-start(bf16[8,1,2,64,128]{4,3,2,1,0:T(8,128)(2,1)S(1)} %get-tuple-element.39), channel_id=1, source_target_pairs={{0,24},{4,12},{8,0},{12,20},{16,8},{20,28},{24,16},{28,4},{1,25},{... | collective-permute-start | bytes 786440 | tf_op jit(solution)/shard_map/ppermute | solution.py:284
  32.3 11.0 %collective-permute-start.6 = (bf16[8,1,2,64,128]{4,3,2,1,0:T(8,128)(2,1)S(1)}, bf16[8,1,2,64,128]{4,3,2,1,0:T(8,128)(2,1)S(1)}, u32[]{:S(2)}, u32[]{:S(2)}) collective-permute-start(bf16[8,1,2,64,128]{4,3,2,1,0:T(8,128)(2,1)S(1)} %add_convert_fusion.3), channel_id=1, source_target_pairs={{0,8},{4,28},{8,16},{12,4},{16,24},{20,12},{24,0},{28,20},{1,9},{5... | collective-permute-start | bytes 786440 | tf_op jit(solution)/shard_map/ppermute | solution.py:278
  34.9 10.7 %collective-permute-start.5 = (bf16[8,1,2,64,128]{4,3,2,1,0:T(8,128)(2,1)S(1)}, bf16[8,1,2,64,128]{4,3,2,1,0:T(8,128)(2,1)S(1)}, u32[]{:S(2)}, u32[]{:S(2)}) collective-permute-start(bf16[8,1,2,64,128]{4,3,2,1,0:T(8,128)(2,1)S(1)} %get-tuple-element.40), channel_id=1, source_target_pairs={{0,4},{4,0},{8,12},{12,8},{16,20},{20,16},{24,28},{28,24},{1,5},{5... | collective-permute-start | bytes 786440 | tf_op jit(solution)/shard_map/ppermute | solution.py:283
  38.5 12.7 %collective-permute-start.7 = (bf16[8,1,2,64,128]{4,3,2,1,0:T(8,128)(2,1)S(1)}, bf16[8,1,2,64,128]{4,3,2,1,0:T(8,128)(2,1)S(1)}, u32[]{:S(2)}, u32[]{:S(2)}) collective-permute-start(bf16[8,1,2,64,128]{4,3,2,1,0:T(8,128)(2,1)S(1)} %get-tuple-element.44), channel_id=1, source_target_pairs={{0,4},{4,0},{8,12},{12,8},{16,20},{20,16},{24,28},{28,24},{1,5},{5... | collective-permute-start | bytes 786440 | tf_op jit(solution)/shard_map/ppermute | solution.py:290
  38.6 12.8 %collective-permute-start.8 = (bf16[8,1,2,64,128]{4,3,2,1,0:T(8,128)(2,1)S(1)}, bf16[8,1,2,64,128]{4,3,2,1,0:T(8,128)(2,1)S(1)}, u32[]{:S(2)}, u32[]{:S(2)}) collective-permute-start(bf16[8,1,2,64,128]{4,3,2,1,0:T(8,128)(2,1)S(1)} %get-tuple-element.45), channel_id=1, source_target_pairs={{0,24},{4,12},{8,0},{12,20},{16,8},{20,28},{24,16},{28,4},{1,25},{... | collective-permute-start | bytes 786440 | tf_op jit(solution)/shard_map/ppermute | solution.py:284
  41.4 14.7 %collective-permute-start.9 = (bf16[8,1,2,64,128]{4,3,2,1,0:T(8,128)(2,1)S(1)}, bf16[8,1,2,64,128]{4,3,2,1,0:T(8,128)(2,1)S(1)}, u32[]{:S(2)}, u32[]{:S(2)}) collective-permute-start(bf16[8,1,2,64,128]{4,3,2,1,0:T(8,128)(2,1)S(1)} %get-tuple-element.46), channel_id=1, source_target_pairs={{0,4},{4,0},{8,12},{12,8},{16,20},{20,16},{24,28},{28,24},{1,5},{5... | collective-permute-start | bytes 786440 | tf_op jit(solution)/shard_map/ppermute | solution.py:290
  45.7 10.4 %collective-permute-start.10 = (bf16[8,1,2,64,128]{4,3,2,1,0:T(8,128)(2,1)S(1)}, bf16[8,1,2,64,128]{4,3,2,1,0:T(8,128)(2,1)S(1)}, u32[]{:S(2)}, u32[]{:S(2)}) collective-permute-start(bf16[8,1,2,64,128]{4,3,2,1,0:T(8,128)(2,1)S(1)} %add_convert_fusion.1), channel_id=1, source_target_pairs={{0,8},{4,28},{8,16},{12,4},{16,24},{20,12},{24,0},{28,20},{1,9},{5... | collective-permute-start | bytes 786440 | tf_op jit(solution)/shard_map/ppermute | solution.py:293

commit v4 on v3

--- a/solution.py
+++ b/solution.py
@@ -112,10 +112,9 @@
                 total[index, atom] += weight_ref[kind * slot_count + entry] * values
             return carry
 
-        count = jnp.int32(0)
-        for slot in range(capacity):
-            count += (atom_ref[owner * capacity + slot] >= 0).astype(jnp.int32)
-        lax.fori_loop(0, count, add, 0)
+        @pl.when(atom_ref[owner * capacity] >= 0)
+        def _():
+            lax.fori_loop(0, capacity, add, 0, unroll=True)
 
     if len(sources) == owner_count:
         for owner, source in enumerate(sources):

time: 57.1 us -> 56.6 us (level)
  waiting for transfers between devices: 26.7 us -> 25.8 us
  transfers between devices with their start and end apart: 12 -> 12, of which waited for: 8 -> 8; matrix products, arithmetic and copies ran while one was open for 1% -> 1% of each run, Pallas kernels for 5% -> 6%
where the time goes in v4:
time: 56.6 us
  waiting for transfers between devices  25.8 us (46%)
  starting transfers between devices  19.9 us (35%)
  Pallas kernels  7.87 us (14%)
  other arithmetic  2.01 us (4%)
  local copies, waits for them, and re-layouts  0.95 us (2%)
    ppermute x2, waiting for transfers between devices, body(): near = lax.ppermute(near, 'energy', inner(1))  9.62 us
    ppermute x3, waiting for transfers between devices, to_owners(): lax.ppermute(blocks[d], 'atom', [(o, o ^ d) for o in range(owner_count)])  8.77 us
    ppermute x2, starting transfers between devices, body(): early = lax.ppermute(early, 'energy', even_odd(-2))  5.87 us
    ppermute x2, waiting for transfers between devices, body(): relay = lax.ppermute(relay, 'energy', inner(1))  5.53 us
    ppermute x2, starting transfers between devices, body(): relay = lax.ppermute(relay, 'energy', inner(1))  5.19 us
    pallas_call x1, Pallas kernels, bond_products(): pl.pallas_call(functools.partial(product_kernel, row_counts, capacity, sp...  4.61 us
    all_to_all x1, starting transfers between devices, to_owners(): lax.all_to_all(blocks, 'atom', split_axis=0, concat_axis=0, tiled=True)  3.51 us
    pallas_call x4, Pallas kernels, atom_sums(): pl.pallas_call(functools.partial(gather_kernel, kinds, owner_count, capac...  3.26 us
  transfers between devices with their start and end apart: 12, of which 8 were waited for; matrix products, arithmetic and copies ran while one was open for 1% of the time, Pallas kernels for 6%

profile of v4, /device:TPU:0, one launch (start us, length us, event | category | flops | bytes accessed | tf_op | source)
XLA Modules:
  0.0 56.6 jit_solution(8174375461093938683)
XLA Ops:
  0.0 0.7 %copy-done = s32[16]{0:T(128)S(1)} copy-done((s32[16]{0:T(128)S(1)}, s32[16]{0:T(128)}, u32[]{:S(2)}) %copy-start) | copy-done | bytes 88
  0.7 4.6 %bond_products.1 = (bf16[32,2,64,128]{3,2,1,0:T(8,128)(2,1)S(1)}, bf16[32,2,64,128]{3,2,1,0:T(8,128)(2,1)}) custom-call(s32[16]{0:T(128)S(1)} %copy-done, bf16[16,1,2,128,128]{4,3,2,1,0:T(8,128)(2,1)} %green_ref.1, bf16[16,3,2,128,128]{4,3,2,1,0:T(8,128)(2,1)} %coupling_ref.1), custom_call_target="tpu_custom_call" | custom-call | flops 1610612736 | bytes 4194304 | tf_op jit(solution)/shard_map/bond_products/pallas_call | solution.py:75
  5.3 0.2 convert_reduce_fusion
  5.9 3.0 %collective-permute-start.1 = (bf16[1040,128]{1,0:T(8,128)(2,1)S(1)}, bf16[1040,128]{1,0:T(8,128)(2,1)S(1)}, u32[]{:S(2)}, u32[]{:S(2)}) collective-permute-start(bf16[1040,128]{1,0:T(8,128)(2,1)S(1)} %get-tuple-element.54), channel_id=1, source_target_pairs={{0,2},{1,3},{2,0},{3,1},{4,6},{5,7},{6,4},{7,5},{8,10},{9,11},{10,... | collective-permute-start | bytes 798728 | tf_op jit(solution)/shard_map/ppermute | solution.py:250
  8.9 0.2 collective-permute-start
  9.1 3.5 %all-to-all-start = ((bf16[4,8,2,64,128]{4,3,2,1,0:T(8,128)(2,1)}), bf16[4,8,2,64,128]{4,3,2,1,0:T(8,128)(2,1)S(1)}, u32[]{:S(2)}, u32[]{:S(2)}) async-start(bf16[4,8,2,64,128]{4,3,2,1,0:T(8,128)(2,1)} %bitcast.16), calls=%async_computation | async-start | bytes 2097152 | tf_op jit(solution)/shard_map/all_to_all | solution.py:244
  12.7 3.5 %collective-permute-done.1.refs_2_ = bf16[1040,128]{1,0:T(8,128)(2,1)S(1)} collective-permute-done((bf16[1040,128]{1,0:T(8,128)(2,1)S(1)}, bf16[1040,128]{1,0:T(8,128)(2,1)S(1)}, u32[]{:S(2)}, u32[]{:S(2)}) %collective-permute-start.1) | collective-permute-done | bytes 266272 | tf_op jit(solution)/shard_map/ppermute | solution.py:250
  16.2 5.3 %collective-permute-done.2.refs_3_ = bf16[1040,128]{1,0:T(8,128)(2,1)S(1)} collective-permute-done((bf16[1040,128]{1,0:T(8,128)(2,1)S(1)}, bf16[1040,128]{1,0:T(8,128)(2,1)S(1)}, u32[]{:S(2)}, u32[]{:S(2)}) %collective-permute-start.2) | collective-permute-done | bytes 266272 | tf_op jit(solution)/shard_map/ppermute | solution.py:250
  21.9 0.8 %atom_sums.5 = (bf16[8,1,2,64,128]{4,3,2,1,0:T(8,128)(2,1)S(1)}, bf16[8,1,2,64,128]{4,3,2,1,0:T(8,128)(2,1)S(1)}) custom-call(s32[32]{0:T(128)S(1)} %add_reduce_fusion.atom_ref, f32[128]{0:T(128)S(1)} %reshape.49.weight_ref, bf16[1040,128]{1,0:T(8,128)(2,1)S(1)} %get-tuple-element.53.refs_0_, bf16[1040,128]{1,0:T(8,128)(2,1)S(1)} %collective-permute-done.refs_1_, ...), custom_call_target="tpu_custom_call" | custom-call | flops 2129920 | bytes 1064960 | tf_op jit(solution)/shard_map/atom_sums/pallas_call | solution.py:138
  22.7 1.6 %collective-permute-start.3 = (bf16[8,1,2,64,128]{4,3,2,1,0:T(8,128)(2,1)S(1)}, bf16[8,1,2,64,128]{4,3,2,1,0:T(8,128)(2,1)S(1)}, u32[]{:S(2)}, u32[]{:S(2)}) collective-permute-start(bf16[8,1,2,64,128]{4,3,2,1,0:T(8,128)(2,1)S(1)} %get-tuple-element.35), channel_id=1, source_target_pairs={{0,4},{4,0},{8,12},{12,8},{16,20},{20,16},{24,28},{28,24},{1,5},{5... | collective-permute-start | bytes 786440 | tf_op jit(solution)/shard_map/ppermute | solution.py:282
  24.3 3.6 %collective-permute-start.4 = (bf16[8,1,2,64,128]{4,3,2,1,0:T(8,128)(2,1)S(1)}, bf16[8,1,2,64,128]{4,3,2,1,0:T(8,128)(2,1)S(1)}, u32[]{:S(2)}, u32[]{:S(2)}) collective-permute-start(bf16[8,1,2,64,128]{4,3,2,1,0:T(8,128)(2,1)S(1)} %get-tuple-element.39), channel_id=1, source_target_pairs={{0,24},{4,12},{8,0},{12,20},{16,8},{20,28},{24,16},{28,4},{1,25},{... | collective-permute-start | bytes 786440 | tf_op jit(solution)/shard_map/ppermute | solution.py:283
  27.9 0.8 %atom_sums.4 = (bf16[8,1,2,64,128]{4,3,2,1,0:T(8,128)(2,1)S(1)}, f32[8,1,2,64,128]{4,3,2,1,0:T(8,128)S(1)}) custom-call(s32[32]{0:T(128)S(1)} %add_reduce_fusion.atom_ref, f32[128]{0:T(128)S(1)} %reshape.49.weight_ref, bf16[1040,128]{1,0:T(8,128)(2,1)S(1)} %get-tuple-element.53.refs_0_, bf16[1040,128]{1,0:T(8,128)(2,1)S(1)} %collective-permute-done.refs_1_, ...), custom_call_target="tpu_custom_call" | custom-call | flops 2129920 | bytes 1064960 | tf_op jit(solution)/shard_map/atom_sums/pallas_call | solution.py:138
  28.7 3.2 %collective-permute-done.3 = bf16[8,1,2,64,128]{4,3,2,1,0:T(8,128)(2,1)S(1)} collective-permute-done((bf16[8,1,2,64,128]{4,3,2,1,0:T(8,128)(2,1)S(1)}, bf16[8,1,2,64,128]{4,3,2,1,0:T(8,128)(2,1)S(1)}, u32[]{:S(2)}, u32[]{:S(2)}) %collective-permute-start.3) | collective-permute-done | bytes 262176 | tf_op jit(solution)/shard_map/ppermute | solution.py:282
  31.9 0.3 all-to-all-done
  32.3 1.8 %collective-permute-start.6 = (bf16[8,1,2,64,128]{4,3,2,1,0:T(8,128)(2,1)S(1)}, bf16[8,1,2,64,128]{4,3,2,1,0:T(8,128)(2,1)S(1)}, u32[]{:S(2)}, u32[]{:S(2)}) collective-permute-start(bf16[8,1,2,64,128]{4,3,2,1,0:T(8,128)(2,1)S(1)} %add_convert_fusion.3), channel_id=1, source_target_pairs={{0,8},{4,28},{8,16},{12,4},{16,24},{20,12},{24,0},{28,20},{1,9},{5... | collective-permute-start | bytes 786440 | tf_op jit(solution)/shard_map/ppermute | solution.py:277
  34.1 0.8 %atom_sums.6 = (bf16[8,1,2,64,128]{4,3,2,1,0:T(8,128)(2,1)S(1)}, bf16[8,1,2,64,128]{4,3,2,1,0:T(8,128)(2,1)S(1)}) custom-call(s32[32]{0:T(128)S(1)} %add_reduce_fusion.atom_ref, f32[128]{0:T(128)S(1)} %reshape.49.weight_ref, bf16[4096,128]{1,0:T(8,128)(2,1)S(1)} %bitcast.30), custom_call_target="tpu_custom_call" | custom-call | flops 2097152 | bytes 1048576 | tf_op jit(solution)/shard_map/atom_sums/pallas_call | solution.py:138
  34.9 3.6 %collective-permute-start.5 = (bf16[8,1,2,64,128]{4,3,2,1,0:T(8,128)(2,1)S(1)}, bf16[8,1,2,64,128]{4,3,2,1,0:T(8,128)(2,1)S(1)}, u32[]{:S(2)}, u32[]{:S(2)}) collective-permute-start(bf16[8,1,2,64,128]{4,3,2,1,0:T(8,128)(2,1)S(1)} %get-tuple-element.40), channel_id=1, source_target_pairs={{0,4},{4,0},{8,12},{12,8},{16,20},{20,16},{24,28},{28,24},{1,5},{5... | collective-permute-start | bytes 786440 | tf_op jit(solution)/shard_map/ppermute | solution.py:282
  38.6 2.3 %collective-permute-start.8 = (bf16[8,1,2,64,128]{4,3,2,1,0:T(8,128)(2,1)S(1)}, bf16[8,1,2,64,128]{4,3,2,1,0:T(8,128)(2,1)S(1)}, u32[]{:S(2)}, u32[]{:S(2)}) collective-permute-start(bf16[8,1,2,64,128]{4,3,2,1,0:T(8,128)(2,1)S(1)} %get-tuple-element.45), channel_id=1, source_target_pairs={{0,24},{4,12},{8,0},{12,20},{16,8},{20,28},{24,16},{28,4},{1,25},{... | collective-permute-start | bytes 786440 | tf_op jit(solution)/shard_map/ppermute | solution.py:283
  40.9 0.8 %atom_sums.7 = (bf16[8,1,2,64,128]{4,3,2,1,0:T(8,128)(2,1)S(1)}, f32[8,1,2,64,128]{4,3,2,1,0:T(8,128)S(1)}) custom-call(s32[32]{0:T(128)S(1)} %add_reduce_fusion.atom_ref, f32[128]{0:T(128)S(1)} %reshape.49.weight_ref, bf16[4096,128]{1,0:T(8,128)(2,1)S(1)} %bitcast.31), custom_call_target="tpu_custom_call" | custom-call | flops 2097152 | bytes 1048576 | tf_op jit(solution)/shard_map/atom_sums/pallas_call | solution.py:138
  41.8 1.5 %collective-permute-done.6 = bf16[8,1,2,64,128]{4,3,2,1,0:T(8,128)(2,1)S(1)} collective-permute-done((bf16[8,1,2,64,128]{4,3,2,1,0:T(8,128)(2,1)S(1)}, bf16[8,1,2,64,128]{4,3,2,1,0:T(8,128)(2,1)S(1)}, u32[]{:S(2)}, u32[]{:S(2)}) %collective-permute-start.6) | collective-permute-done | bytes 262176 | tf_op jit(solution)/shard_map/ppermute | solution.py:277
  43.4 2.4 %collective-permute-done.5 = bf16[8,1,2,64,128]{4,3,2,1,0:T(8,128)(2,1)S(1)} collective-permute-done((bf16[8,1,2,64,128]{4,3,2,1,0:T(8,128)(2,1)S(1)}, bf16[8,1,2,64,128]{4,3,2,1,0:T(8,128)(2,1)S(1)}, u32[]{:S(2)}, u32[]{:S(2)}) %collective-permute-start.5) | collective-permute-done | bytes 262176 | tf_op jit(solution)/shard_map/ppermute | solution.py:282
  45.9 5.4 %collective-permute-done.7 = bf16[8,1,2,64,128]{4,3,2,1,0:T(8,128)(2,1)S(1)} collective-permute-done((bf16[8,1,2,64,128]{4,3,2,1,0:T(8,128)(2,1)S(1)}, bf16[8,1,2,64,128]{4,3,2,1,0:T(8,128)(2,1)S(1)}, u32[]{:S(2)}, u32[]{:S(2)}) %collective-permute-start.7) | collective-permute-done | bytes 262176 | tf_op jit(solution)/shard_map/ppermute | solution.py:289
  51.5 4.2 %collective-permute-done.9 = bf16[8,1,2,64,128]{4,3,2,1,0:T(8,128)(2,1)S(1)} collective-permute-done((bf16[8,1,2,64,128]{4,3,2,1,0:T(8,128)(2,1)S(1)}, bf16[8,1,2,64,128]{4,3,2,1,0:T(8,128)(2,1)S(1)}, u32[]{:S(2)}, u32[]{:S(2)}) %collective-permute-start.9) | collective-permute-done | bytes 262176 | tf_op jit(solution)/shard_map/ppermute | solution.py:289
  55.8 0.8 %pad_maximum_fusion = bf16[8,1,2,128,128]{4,3,2,1,0:T(8,128)(2,1)} fusion(bf16[8,1,2,64,128]{4,3,2,1,0:T(8,128)(2,1)S(1)} %add_convert_fusion, bf16[8,1,2,64,128]{4,3,2,1,0:T(8,128)(2,1)S(1)} %add_convert_fusion.2), kind=kLoop, calls=%fused_computation.6 | loop fusion | flops 1048576 | bytes 1048576 | tf_op jit(solution)/shard_map/concatenate | solution.py:308
  (37 shorter events, 1.6 us)
Async XLA Ops:
  0.0 0.7 %copy-start = (s32[16]{0:T(128)S(1)}, s32[16]{0:T(128)}, u32[]{:S(2)}) copy-start(s32[16]{0:T(128)} %atom_ref.1) | copy-start | bytes 196
  0.7 4.9 %copy-start.1 = (f32[2,16,2]{1,2,0:T(2,128)S(1)}, f32[2,16,2]{1,2,0:T(2,128)}, u32[]{:S(2)}) copy-start(f32[2,16,2]{1,2,0:T(2,128)} %param.7) | copy-start | bytes 772
  0.7 4.9 %copy-start.2 = (s32[16,2]{0,1:T(2,128)S(1)}, s32[16,2]{0,1:T(2,128)}, u32[]{:S(2)}) copy-start(s32[16,2]{0,1:T(2,128)} %param.8) | copy-start | bytes 388
  5.9 10.2 %collective-permute-start.1 = (bf16[1040,128]{1,0:T(8,128)(2,1)S(1)}, bf16[1040,128]{1,0:T(8,128)(2,1)S(1)}, u32[]{:S(2)}, u32[]{:S(2)}) collective-permute-start(bf16[1040,128]{1,0:T(8,128)(2,1)S(1)} %get-tuple-element.54), channel_id=1, source_target_pairs={{0,2},{1,3},{2,0},{3,1},{4,6},{5,7},{6,4},{7,5},{8,10},{9,11},{10,... | collective-permute-start | bytes 798728 | tf_op jit(solution)/shard_map/ppermute | solution.py:250
  8.9 12.5 %collective-permute-start.2 = (bf16[1040,128]{1,0:T(8,128)(2,1)S(1)}, bf16[1040,128]{1,0:T(8,128)(2,1)S(1)}, u32[]{:S(2)}, u32[]{:S(2)}) collective-permute-start(bf16[1040,128]{1,0:T(8,128)(2,1)S(1)} %get-tuple-element.55), channel_id=1, source_target_pairs={{0,3},{1,2},{2,1},{3,0},{4,7},{5,6},{6,5},{7,4},{8,11},{9,10},{10,... | collective-permute-start | bytes 798728 | tf_op jit(solution)/shard_map/ppermute | solution.py:250
  8.9 12.5 %collective-permute-start = (bf16[1040,128]{1,0:T(8,128)(2,1)S(1)}, bf16[1040,128]{1,0:T(8,128)(2,1)S(1)}, u32[]{:S(2)}, u32[]{:S(2)}) collective-permute-start(bf16[1040,128]{1,0:T(8,128)(2,1)S(1)} %get-tuple-element.56), channel_id=1, source_target_pairs={{0,1},{1,0},{2,3},{3,2},{4,5},{5,4},{6,7},{7,6},{8,9},{9,8},{10,11... | collective-permute-start | bytes 798728 | tf_op jit(solution)/shard_map/ppermute | solution.py:250
  9.1 23.1 %all-to-all-start = ((bf16[4,8,2,64,128]{4,3,2,1,0:T(8,128)(2,1)}), bf16[4,8,2,64,128]{4,3,2,1,0:T(8,128)(2,1)S(1)}, u32[]{:S(2)}, u32[]{:S(2)}) async-start(bf16[4,8,2,64,128]{4,3,2,1,0:T(8,128)(2,1)} %bitcast.16), calls=%async_computation | async-start | bytes 2097152 | tf_op jit(solution)/shard_map/all_to_all | solution.py:244
  22.7 9.2 %collective-permute-start.3 = (bf16[8,1,2,64,128]{4,3,2,1,0:T(8,128)(2,1)S(1)}, bf16[8,1,2,64,128]{4,3,2,1,0:T(8,128)(2,1)S(1)}, u32[]{:S(2)}, u32[]{:S(2)}) collective-permute-start(bf16[8,1,2,64,128]{4,3,2,1,0:T(8,128)(2,1)S(1)} %get-tuple-element.35), channel_id=1, source_target_pairs={{0,4},{4,0},{8,12},{12,8},{16,20},{20,16},{24,28},{28,24},{1,5},{5... | collective-permute-start | bytes 786440 | tf_op jit(solution)/shard_map/ppermute | solution.py:282
  24.3 10.6 %collective-permute-start.4 = (bf16[8,1,2,64,128]{4,3,2,1,0:T(8,128)(2,1)S(1)}, bf16[8,1,2,64,128]{4,3,2,1,0:T(8,128)(2,1)S(1)}, u32[]{:S(2)}, u32[]{:S(2)}) collective-permute-start(bf16[8,1,2,64,128]{4,3,2,1,0:T(8,128)(2,1)S(1)} %get-tuple-element.39), channel_id=1, source_target_pairs={{0,24},{4,12},{8,0},{12,20},{16,8},{20,28},{24,16},{28,4},{1,25},{... | collective-permute-start | bytes 786440 | tf_op jit(solution)/shard_map/ppermute | solution.py:283
  32.3 11.0 %collective-permute-start.6 = (bf16[8,1,2,64,128]{4,3,2,1,0:T(8,128)(2,1)S(1)}, bf16[8,1,2,64,128]{4,3,2,1,0:T(8,128)(2,1)S(1)}, u32[]{:S(2)}, u32[]{:S(2)}) collective-permute-start(bf16[8,1,2,64,128]{4,3,2,1,0:T(8,128)(2,1)S(1)} %add_convert_fusion.3), channel_id=1, source_target_pairs={{0,8},{4,28},{8,16},{12,4},{16,24},{20,12},{24,0},{28,20},{1,9},{5... | collective-permute-start | bytes 786440 | tf_op jit(solution)/shard_map/ppermute | solution.py:277
  34.9 10.8 %collective-permute-start.5 = (bf16[8,1,2,64,128]{4,3,2,1,0:T(8,128)(2,1)S(1)}, bf16[8,1,2,64,128]{4,3,2,1,0:T(8,128)(2,1)S(1)}, u32[]{:S(2)}, u32[]{:S(2)}) collective-permute-start(bf16[8,1,2,64,128]{4,3,2,1,0:T(8,128)(2,1)S(1)} %get-tuple-element.40), channel_id=1, source_target_pairs={{0,4},{4,0},{8,12},{12,8},{16,20},{20,16},{24,28},{28,24},{1,5},{5... | collective-permute-start | bytes 786440 | tf_op jit(solution)/shard_map/ppermute | solution.py:282
  38.5 12.8 %collective-permute-start.7 = (bf16[8,1,2,64,128]{4,3,2,1,0:T(8,128)(2,1)S(1)}, bf16[8,1,2,64,128]{4,3,2,1,0:T(8,128)(2,1)S(1)}, u32[]{:S(2)}, u32[]{:S(2)}) collective-permute-start(bf16[8,1,2,64,128]{4,3,2,1,0:T(8,128)(2,1)S(1)} %get-tuple-element.44), channel_id=1, source_target_pairs={{0,4},{4,0},{8,12},{12,8},{16,20},{20,16},{24,28},{28,24},{1,5},{5... | collective-permute-start | bytes 786440 | tf_op jit(solution)/shard_map/ppermute | solution.py:289
  38.6 12.8 %collective-permute-start.8 = (bf16[8,1,2,64,128]{4,3,2,1,0:T(8,128)(2,1)S(1)}, bf16[8,1,2,64,128]{4,3,2,1,0:T(8,128)(2,1)S(1)}, u32[]{:S(2)}, u32[]{:S(2)}) collective-permute-start(bf16[8,1,2,64,128]{4,3,2,1,0:T(8,128)(2,1)S(1)} %get-tuple-element.45), channel_id=1, source_target_pairs={{0,24},{4,12},{8,0},{12,20},{16,8},{20,28},{24,16},{28,4},{1,25},{... | collective-permute-start | bytes 786440 | tf_op jit(solution)/shard_map/ppermute | solution.py:283
  41.7 13.9 %collective-permute-start.9 = (bf16[8,1,2,64,128]{4,3,2,1,0:T(8,128)(2,1)S(1)}, bf16[8,1,2,64,128]{4,3,2,1,0:T(8,128)(2,1)S(1)}, u32[]{:S(2)}, u32[]{:S(2)}) collective-permute-start(bf16[8,1,2,64,128]{4,3,2,1,0:T(8,128)(2,1)S(1)} %get-tuple-element.46), channel_id=1, source_target_pairs={{0,4},{4,0},{8,12},{12,8},{16,20},{20,16},{24,28},{28,24},{1,5},{5... | collective-permute-start | bytes 786440 | tf_op jit(solution)/shard_map/ppermute | solution.py:289
  45.8 9.8 %collective-permute-start.10 = (bf16[8,1,2,64,128]{4,3,2,1,0:T(8,128)(2,1)S(1)}, bf16[8,1,2,64,128]{4,3,2,1,0:T(8,128)(2,1)S(1)}, u32[]{:S(2)}, u32[]{:S(2)}) collective-permute-start(bf16[8,1,2,64,128]{4,3,2,1,0:T(8,128)(2,1)S(1)} %add_convert_fusion.1), channel_id=1, source_target_pairs={{0,8},{4,28},{8,16},{12,4},{16,24},{20,12},{24,0},{28,20},{1,9},{5... | collective-permute-start | bytes 786440 | tf_op jit(solution)/shard_map/ppermute | solution.py:292

commit v5 on v4

--- a/solution.py
+++ b/solution.py
@@ -24,7 +24,7 @@
         for owner in range(used_ref.shape[0]):
             used_ref[owner] = 0
 
-    products = []
+    products, lasts = [], []
     for index in range(group):
         real_green = green_ref[index, 0, 0]
         imag_green = green_ref[index, 0, 1]
@@ -46,15 +46,15 @@
         products.append(
             jnp.concatenate([product[c * size : (c + 1) * size] for c in range(components)], axis=1)
         )
-    for index in range(group):
         rows_of = []
         for c in range(components):
             real_last, imag_last = coupling_ref[index, c, 0].T, coupling_ref[index, c, 1].T
             rows_of.append(jnp.concatenate([real_last, imag_last], axis=1))
             rows_of.append(jnp.concatenate([-imag_last, real_last], axis=1))
-        last = jnp.concatenate(rows_of, axis=0)
+        lasts.append(jnp.concatenate(rows_of, axis=0))
+    for index in range(group):
         total = lax.dot_general(
-            products[index], last, (((1,), (0,)), ((), ())), preferred_element_type=jnp.float32
+            products[index], lasts[index], (((1,), (0,)), ((), ())), preferred_element_type=jnp.float32
         ).astype(jnp.bfloat16)
         owner = lax.div(atom_ref[step * group + index], A_DEV)
         rank = used_ref[owner]
@@ -277,7 +277,7 @@
                 parts[-1][2] = lax.ppermute(merged, "energy", even_odd(2))
             relay, early = sums_of(c, (1, 2))
             if c > 0:
-                relay, early, parts[-1][0] = lax.optimization_barrier((relay, early, parts[-1][0]))
+                early, parts[-1][0] = lax.optimization_barrier((early, parts[-1][0]))
             near, late = sums_of(c, (0, 3))
             relay = lax.ppermute(relay, "energy", inner(1))
             early = lax.ppermute(early, "energy", even_odd(-2))

time: 56.6 us -> 57 us (level)
    ppermute x2, starting transfers between devices: 5.87 us -> 4.04 us  [body(): early = lax.ppermute(early, 'energy', even_odd(-2))]
    ppermute x2, starting transfers between devices: 0.15 us -> 1.65 us  [body(): near = lax.ppermute(near, 'energy', inner(1))]
where the time goes in v5:
time: 57 us; the launch traced here: 56.6 us
  waiting for transfers between devices  26.1 us (46%)
  starting transfers between devices  19.6 us (34%)
  Pallas kernels  7.88 us (14%)
  other arithmetic  2.01 us (4%)
  local copies, waits for them, and re-layouts  0.95 us (2%)
    ppermute x2, waiting for transfers between devices, body(): near = lax.ppermute(near, 'energy', inner(1))  9.61 us
    ppermute x3, waiting for transfers between devices, to_owners(): lax.ppermute(blocks[d], 'atom', [(o, o ^ d) for o in range(owner_count)])  8.78 us
    ppermute x2, waiting for transfers between devices, body(): relay = lax.ppermute(relay, 'energy', inner(1))  5.51 us
    ppermute x2, starting transfers between devices, body(): relay = lax.ppermute(relay, 'energy', inner(1))  5.2 us
    pallas_call x1, Pallas kernels, bond_products(): pl.pallas_call(functools.partial(product_kernel, row_counts, capacity, sp...  4.62 us
    ppermute x2, starting transfers between devices, body(): early = lax.ppermute(early, 'energy', even_odd(-2))  4.04 us
    all_to_all x1, starting transfers between devices, to_owners(): lax.all_to_all(blocks, 'atom', split_axis=0, concat_axis=0, tiled=True)  3.51 us
    pallas_call x4, Pallas kernels, atom_sums(): pl.pallas_call(functools.partial(gather_kernel, kinds, owner_count, capac...  3.26 us
  transfers between devices with their start and end apart: 12, of which 8 were waited for; matrix products, arithmetic and copies ran while one was open for 1% of the time, Pallas kernels for 6%

profile of v5, /device:TPU:0, one launch (start us, length us, event | category | flops | bytes accessed | tf_op | source)
XLA Modules:
  0.0 56.6 jit_solution(13480545582897850233)
XLA Ops:
  0.0 0.7 %copy-done = s32[16]{0:T(128)S(1)} copy-done((s32[16]{0:T(128)S(1)}, s32[16]{0:T(128)}, u32[]{:S(2)}) %copy-start) | copy-done | bytes 88
  0.7 4.6 %bond_products.1 = (bf16[32,2,64,128]{3,2,1,0:T(8,128)(2,1)S(1)}, bf16[32,2,64,128]{3,2,1,0:T(8,128)(2,1)}) custom-call(s32[16]{0:T(128)S(1)} %copy-done, bf16[16,1,2,128,128]{4,3,2,1,0:T(8,128)(2,1)} %green_ref.1, bf16[16,3,2,128,128]{4,3,2,1,0:T(8,128)(2,1)} %coupling_ref.1), custom_call_target="tpu_custom_call" | custom-call | flops 1610612736 | bytes 4194304 | tf_op jit(solution)/shard_map/bond_products/pallas_call | solution.py:75
  5.9 3.0 %collective-permute-start.1 = (bf16[1040,128]{1,0:T(8,128)(2,1)S(1)}, bf16[1040,128]{1,0:T(8,128)(2,1)S(1)}, u32[]{:S(2)}, u32[]{:S(2)}) collective-permute-start(bf16[1040,128]{1,0:T(8,128)(2,1)S(1)} %get-tuple-element.52), channel_id=1, source_target_pairs={{0,2},{1,3},{2,0},{3,1},{4,6},{5,7},{6,4},{7,5},{8,10},{9,11},{10,... | collective-permute-start | bytes 798728 | tf_op jit(solution)/shard_map/ppermute | solution.py:250
  9.0 0.2 collective-permute-start
  9.1 3.5 %all-to-all-start = ((bf16[4,8,2,64,128]{4,3,2,1,0:T(8,128)(2,1)}), bf16[4,8,2,64,128]{4,3,2,1,0:T(8,128)(2,1)S(1)}, u32[]{:S(2)}, u32[]{:S(2)}) async-start(bf16[4,8,2,64,128]{4,3,2,1,0:T(8,128)(2,1)} %bitcast.16), calls=%async_computation | async-start | bytes 2097152 | tf_op jit(solution)/shard_map/all_to_all | solution.py:244
  12.7 3.5 %collective-permute-done.1.refs_2_ = bf16[1040,128]{1,0:T(8,128)(2,1)S(1)} collective-permute-done((bf16[1040,128]{1,0:T(8,128)(2,1)S(1)}, bf16[1040,128]{1,0:T(8,128)(2,1)S(1)}, u32[]{:S(2)}, u32[]{:S(2)}) %collective-permute-start.1) | collective-permute-done | bytes 266272 | tf_op jit(solution)/shard_map/ppermute | solution.py:250
  16.2 5.3 %collective-permute-done.2.refs_3_ = bf16[1040,128]{1,0:T(8,128)(2,1)S(1)} collective-permute-done((bf16[1040,128]{1,0:T(8,128)(2,1)S(1)}, bf16[1040,128]{1,0:T(8,128)(2,1)S(1)}, u32[]{:S(2)}, u32[]{:S(2)}) %collective-permute-start.2) | collective-permute-done | bytes 266272 | tf_op jit(solution)/shard_map/ppermute | solution.py:250
  21.9 0.8 %atom_sums.5 = (bf16[8,1,2,64,128]{4,3,2,1,0:T(8,128)(2,1)S(1)}, bf16[8,1,2,64,128]{4,3,2,1,0:T(8,128)(2,1)S(1)}) custom-call(s32[32]{0:T(128)S(1)} %add_reduce_fusion.atom_ref, f32[128]{0:T(128)S(1)} %reshape.49.weight_ref, bf16[1040,128]{1,0:T(8,128)(2,1)S(1)} %get-tuple-element.51.refs_0_, bf16[1040,128]{1,0:T(8,128)(2,1)S(1)} %collective-permute-done.refs_1_, ...), custom_call_target="tpu_custom_call" | custom-call | flops 2129920 | bytes 1064960 | tf_op jit(solution)/shard_map/atom_sums/pallas_call | solution.py:138
  22.7 1.6 %collective-permute-start.3 = (bf16[8,1,2,64,128]{4,3,2,1,0:T(8,128)(2,1)S(1)}, bf16[8,1,2,64,128]{4,3,2,1,0:T(8,128)(2,1)S(1)}, u32[]{:S(2)}, u32[]{:S(2)}) collective-permute-start(bf16[8,1,2,64,128]{4,3,2,1,0:T(8,128)(2,1)S(1)} %get-tuple-element.34), channel_id=1, source_target_pairs={{0,4},{4,0},{8,12},{12,8},{16,20},{20,16},{24,28},{28,24},{1,5},{5... | collective-permute-start | bytes 786440 | tf_op jit(solution)/shard_map/ppermute | solution.py:282
  24.3 3.6 %collective-permute-start.5 = (bf16[8,1,2,64,128]{4,3,2,1,0:T(8,128)(2,1)S(1)}, bf16[8,1,2,64,128]{4,3,2,1,0:T(8,128)(2,1)S(1)}, u32[]{:S(2)}, u32[]{:S(2)}) collective-permute-start(bf16[8,1,2,64,128]{4,3,2,1,0:T(8,128)(2,1)S(1)} %get-tuple-element.38), channel_id=1, source_target_pairs={{0,24},{4,12},{8,0},{12,20},{16,8},{20,28},{24,16},{28,4},{1,25},{... | collective-permute-start | bytes 786440 | tf_op jit(solution)/shard_map/ppermute | solution.py:283
  27.9 0.8 %atom_sums.4 = (bf16[8,1,2,64,128]{4,3,2,1,0:T(8,128)(2,1)S(1)}, f32[8,1,2,64,128]{4,3,2,1,0:T(8,128)S(1)}) custom-call(s32[32]{0:T(128)S(1)} %add_reduce_fusion.atom_ref, f32[128]{0:T(128)S(1)} %reshape.49.weight_ref, bf16[1040,128]{1,0:T(8,128)(2,1)S(1)} %get-tuple-element.51.refs_0_, bf16[1040,128]{1,0:T(8,128)(2,1)S(1)} %collective-permute-done.refs_1_, ...), custom_call_target="tpu_custom_call" | custom-call | flops 2129920 | bytes 1064960 | tf_op jit(solution)/shard_map/atom_sums/pallas_call | solution.py:138
  28.7 3.2 %collective-permute-done.3 = bf16[8,1,2,64,128]{4,3,2,1,0:T(8,128)(2,1)S(1)} collective-permute-done((bf16[8,1,2,64,128]{4,3,2,1,0:T(8,128)(2,1)S(1)}, bf16[8,1,2,64,128]{4,3,2,1,0:T(8,128)(2,1)S(1)}, u32[]{:S(2)}, u32[]{:S(2)}) %collective-permute-start.3) | collective-permute-done | bytes 262176 | tf_op jit(solution)/shard_map/ppermute | solution.py:282
  31.9 0.3 all-to-all-done
  32.3 1.8 %collective-permute-start.6 = (bf16[8,1,2,64,128]{4,3,2,1,0:T(8,128)(2,1)S(1)}, bf16[8,1,2,64,128]{4,3,2,1,0:T(8,128)(2,1)S(1)}, u32[]{:S(2)}, u32[]{:S(2)}) collective-permute-start(bf16[8,1,2,64,128]{4,3,2,1,0:T(8,128)(2,1)S(1)} %add_convert_fusion.3), channel_id=1, source_target_pairs={{0,8},{4,28},{8,16},{12,4},{16,24},{20,12},{24,0},{28,20},{1,9},{5... | collective-permute-start | bytes 786440 | tf_op jit(solution)/shard_map/ppermute | solution.py:277
  34.1 0.8 %atom_sums.6 = (bf16[8,1,2,64,128]{4,3,2,1,0:T(8,128)(2,1)S(1)}, bf16[8,1,2,64,128]{4,3,2,1,0:T(8,128)(2,1)S(1)}) custom-call(s32[32]{0:T(128)S(1)} %add_reduce_fusion.atom_ref, f32[128]{0:T(128)S(1)} %reshape.49.weight_ref, bf16[4096,128]{1,0:T(8,128)(2,1)S(1)} %bitcast.30), custom_call_target="tpu_custom_call" | custom-call | flops 2097152 | bytes 1048576 | tf_op jit(solution)/shard_map/atom_sums/pallas_call | solution.py:138
  34.9 3.6 %collective-permute-start.4 = (bf16[8,1,2,64,128]{4,3,2,1,0:T(8,128)(2,1)S(1)}, bf16[8,1,2,64,128]{4,3,2,1,0:T(8,128)(2,1)S(1)}, u32[]{:S(2)}, u32[]{:S(2)}) collective-permute-start(bf16[8,1,2,64,128]{4,3,2,1,0:T(8,128)(2,1)S(1)} %get-tuple-element.36), channel_id=1, source_target_pairs={{0,4},{4,0},{8,12},{12,8},{16,20},{20,16},{24,28},{28,24},{1,5},{5... | collective-permute-start | bytes 786440 | tf_op jit(solution)/shard_map/ppermute | solution.py:282
  38.6 0.4 collective-permute-start.8
  39.1 0.8 %atom_sums.7 = (bf16[8,1,2,64,128]{4,3,2,1,0:T(8,128)(2,1)S(1)}, f32[8,1,2,64,128]{4,3,2,1,0:T(8,128)S(1)}) custom-call(s32[32]{0:T(128)S(1)} %add_reduce_fusion.atom_ref, f32[128]{0:T(128)S(1)} %reshape.49.weight_ref, bf16[4096,128]{1,0:T(8,128)(2,1)S(1)} %bitcast.31), custom_call_target="tpu_custom_call" | custom-call | flops 2097152 | bytes 1048576 | tf_op jit(solution)/shard_map/atom_sums/pallas_call | solution.py:138
  39.9 1.6 %collective-permute-start.9 = (bf16[8,1,2,64,128]{4,3,2,1,0:T(8,128)(2,1)S(1)}, bf16[8,1,2,64,128]{4,3,2,1,0:T(8,128)(2,1)S(1)}, u32[]{:S(2)}, u32[]{:S(2)}) collective-permute-start(bf16[8,1,2,64,128]{4,3,2,1,0:T(8,128)(2,1)S(1)} %get-tuple-element.44), channel_id=1, source_target_pairs={{0,4},{4,0},{8,12},{12,8},{16,20},{20,16},{24,28},{28,24},{1,5},{5... | collective-permute-start | bytes 786440 | tf_op jit(solution)/shard_map/ppermute | solution.py:289
  41.5 1.8 %collective-permute-done.6 = bf16[8,1,2,64,128]{4,3,2,1,0:T(8,128)(2,1)S(1)} collective-permute-done((bf16[8,1,2,64,128]{4,3,2,1,0:T(8,128)(2,1)S(1)}, bf16[8,1,2,64,128]{4,3,2,1,0:T(8,128)(2,1)S(1)}, u32[]{:S(2)}, u32[]{:S(2)}) %collective-permute-start.6) | collective-permute-done | bytes 262176 | tf_op jit(solution)/shard_map/ppermute | solution.py:277
  43.4 2.4 %collective-permute-done.4 = bf16[8,1,2,64,128]{4,3,2,1,0:T(8,128)(2,1)S(1)} collective-permute-done((bf16[8,1,2,64,128]{4,3,2,1,0:T(8,128)(2,1)S(1)}, bf16[8,1,2,64,128]{4,3,2,1,0:T(8,128)(2,1)S(1)}, u32[]{:S(2)}, u32[]{:S(2)}) %collective-permute-start.4) | collective-permute-done | bytes 262176 | tf_op jit(solution)/shard_map/ppermute | solution.py:282
  46.0 5.4 %collective-permute-done.7 = bf16[8,1,2,64,128]{4,3,2,1,0:T(8,128)(2,1)S(1)} collective-permute-done((bf16[8,1,2,64,128]{4,3,2,1,0:T(8,128)(2,1)S(1)}, bf16[8,1,2,64,128]{4,3,2,1,0:T(8,128)(2,1)S(1)}, u32[]{:S(2)}, u32[]{:S(2)}) %collective-permute-start.7) | collective-permute-done | bytes 262176 | tf_op jit(solution)/shard_map/ppermute | solution.py:289
  51.5 4.2 %collective-permute-done.9 = bf16[8,1,2,64,128]{4,3,2,1,0:T(8,128)(2,1)S(1)} collective-permute-done((bf16[8,1,2,64,128]{4,3,2,1,0:T(8,128)(2,1)S(1)}, bf16[8,1,2,64,128]{4,3,2,1,0:T(8,128)(2,1)S(1)}, u32[]{:S(2)}, u32[]{:S(2)}) %collective-permute-start.9) | collective-permute-done | bytes 262176 | tf_op jit(solution)/shard_map/ppermute | solution.py:289
  55.8 0.8 %pad_maximum_fusion = bf16[8,1,2,128,128]{4,3,2,1,0:T(8,128)(2,1)} fusion(bf16[8,1,2,64,128]{4,3,2,1,0:T(8,128)(2,1)S(1)} %add_convert_fusion, bf16[8,1,2,64,128]{4,3,2,1,0:T(8,128)(2,1)S(1)} %add_convert_fusion.2), kind=kLoop, calls=%fused_computation.6 | loop fusion | flops 1048576 | bytes 1048576 | tf_op jit(solution)/shard_map/concatenate | solution.py:308
  (37 shorter events, 1.7 us)
Async XLA Ops:
  0.0 0.7 %copy-start = (s32[16]{0:T(128)S(1)}, s32[16]{0:T(128)}, u32[]{:S(2)}) copy-start(s32[16]{0:T(128)} %atom_ref.1) | copy-start | bytes 196
  0.7 4.9 %copy-start.1 = (f32[2,16,2]{1,2,0:T(2,128)S(1)}, f32[2,16,2]{1,2,0:T(2,128)}, u32[]{:S(2)}) copy-start(f32[2,16,2]{1,2,0:T(2,128)} %param.7) | copy-start | bytes 772
  0.7 4.9 %copy-start.2 = (s32[16,2]{0,1:T(2,128)S(1)}, s32[16,2]{0,1:T(2,128)}, u32[]{:S(2)}) copy-start(s32[16,2]{0,1:T(2,128)} %param.8) | copy-start | bytes 388
  5.9 10.2 %collective-permute-start.1 = (bf16[1040,128]{1,0:T(8,128)(2,1)S(1)}, bf16[1040,128]{1,0:T(8,128)(2,1)S(1)}, u32[]{:S(2)}, u32[]{:S(2)}) collective-permute-start(bf16[1040,128]{1,0:T(8,128)(2,1)S(1)} %get-tuple-element.52), channel_id=1, source_target_pairs={{0,2},{1,3},{2,0},{3,1},{4,6},{5,7},{6,4},{7,5},{8,10},{9,11},{10,... | collective-permute-start | bytes 798728 | tf_op jit(solution)/shard_map/ppermute | solution.py:250
  8.9 12.5 %collective-permute-start.2 = (bf16[1040,128]{1,0:T(8,128)(2,1)S(1)}, bf16[1040,128]{1,0:T(8,128)(2,1)S(1)}, u32[]{:S(2)}, u32[]{:S(2)}) collective-permute-start(bf16[1040,128]{1,0:T(8,128)(2,1)S(1)} %get-tuple-element.53), channel_id=1, source_target_pairs={{0,3},{1,2},{2,1},{3,0},{4,7},{5,6},{6,5},{7,4},{8,11},{9,10},{10,... | collective-permute-start | bytes 798728 | tf_op jit(solution)/shard_map/ppermute | solution.py:250
  9.0 12.5 %collective-permute-start = (bf16[1040,128]{1,0:T(8,128)(2,1)S(1)}, bf16[1040,128]{1,0:T(8,128)(2,1)S(1)}, u32[]{:S(2)}, u32[]{:S(2)}) collective-permute-start(bf16[1040,128]{1,0:T(8,128)(2,1)S(1)} %get-tuple-element.54), channel_id=1, source_target_pairs={{0,1},{1,0},{2,3},{3,2},{4,5},{5,4},{6,7},{7,6},{8,9},{9,8},{10,11... | collective-permute-start | bytes 798728 | tf_op jit(solution)/shard_map/ppermute | solution.py:250
  9.1 23.1 %all-to-all-start = ((bf16[4,8,2,64,128]{4,3,2,1,0:T(8,128)(2,1)}), bf16[4,8,2,64,128]{4,3,2,1,0:T(8,128)(2,1)S(1)}, u32[]{:S(2)}, u32[]{:S(2)}) async-start(bf16[4,8,2,64,128]{4,3,2,1,0:T(8,128)(2,1)} %bitcast.16), calls=%async_computation | async-start | bytes 2097152 | tf_op jit(solution)/shard_map/all_to_all | solution.py:244
  22.7 9.2 %collective-permute-start.3 = (bf16[8,1,2,64,128]{4,3,2,1,0:T(8,128)(2,1)S(1)}, bf16[8,1,2,64,128]{4,3,2,1,0:T(8,128)(2,1)S(1)}, u32[]{:S(2)}, u32[]{:S(2)}) collective-permute-start(bf16[8,1,2,64,128]{4,3,2,1,0:T(8,128)(2,1)S(1)} %get-tuple-element.34), channel_id=1, source_target_pairs={{0,4},{4,0},{8,12},{12,8},{16,20},{20,16},{24,28},{28,24},{1,5},{5... | collective-permute-start | bytes 786440 | tf_op jit(solution)/shard_map/ppermute | solution.py:282
  24.3 14.3 %collective-permute-start.5 = (bf16[8,1,2,64,128]{4,3,2,1,0:T(8,128)(2,1)S(1)}, bf16[8,1,2,64,128]{4,3,2,1,0:T(8,128)(2,1)S(1)}, u32[]{:S(2)}, u32[]{:S(2)}) collective-permute-start(bf16[8,1,2,64,128]{4,3,2,1,0:T(8,128)(2,1)S(1)} %get-tuple-element.38), channel_id=1, source_target_pairs={{0,24},{4,12},{8,0},{12,20},{16,8},{20,28},{24,16},{28,4},{1,25},{... | collective-permute-start | bytes 786440 | tf_op jit(solution)/shard_map/ppermute | solution.py:283
  32.3 11.0 %collective-permute-start.6 = (bf16[8,1,2,64,128]{4,3,2,1,0:T(8,128)(2,1)S(1)}, bf16[8,1,2,64,128]{4,3,2,1,0:T(8,128)(2,1)S(1)}, u32[]{:S(2)}, u32[]{:S(2)}) collective-permute-start(bf16[8,1,2,64,128]{4,3,2,1,0:T(8,128)(2,1)S(1)} %add_convert_fusion.3), channel_id=1, source_target_pairs={{0,8},{4,28},{8,16},{12,4},{16,24},{20,12},{24,0},{28,20},{1,9},{5... | collective-permute-start | bytes 786440 | tf_op jit(solution)/shard_map/ppermute | solution.py:277
  34.9 10.8 %collective-permute-start.4 = (bf16[8,1,2,64,128]{4,3,2,1,0:T(8,128)(2,1)S(1)}, bf16[8,1,2,64,128]{4,3,2,1,0:T(8,128)(2,1)S(1)}, u32[]{:S(2)}, u32[]{:S(2)}) collective-permute-start(bf16[8,1,2,64,128]{4,3,2,1,0:T(8,128)(2,1)S(1)} %get-tuple-element.36), channel_id=1, source_target_pairs={{0,4},{4,0},{8,12},{12,8},{16,20},{20,16},{24,28},{28,24},{1,5},{5... | collective-permute-start | bytes 786440 | tf_op jit(solution)/shard_map/ppermute | solution.py:282
  38.6 12.8 %collective-permute-start.7 = (bf16[8,1,2,64,128]{4,3,2,1,0:T(8,128)(2,1)S(1)}, bf16[8,1,2,64,128]{4,3,2,1,0:T(8,128)(2,1)S(1)}, u32[]{:S(2)}, u32[]{:S(2)}) collective-permute-start(bf16[8,1,2,64,128]{4,3,2,1,0:T(8,128)(2,1)S(1)} %get-tuple-element.42), channel_id=1, source_target_pairs={{0,4},{4,0},{8,12},{12,8},{16,20},{20,16},{24,28},{28,24},{1,5},{5... | collective-permute-start | bytes 786440 | tf_op jit(solution)/shard_map/ppermute | solution.py:289
  38.6 12.8 %collective-permute-start.8 = (bf16[8,1,2,64,128]{4,3,2,1,0:T(8,128)(2,1)S(1)}, bf16[8,1,2,64,128]{4,3,2,1,0:T(8,128)(2,1)S(1)}, u32[]{:S(2)}, u32[]{:S(2)}) collective-permute-start(bf16[8,1,2,64,128]{4,3,2,1,0:T(8,128)(2,1)S(1)} %get-tuple-element.43), channel_id=1, source_target_pairs={{0,24},{4,12},{8,0},{12,20},{16,8},{20,28},{24,16},{28,4},{1,25},{... | collective-permute-start | bytes 786440 | tf_op jit(solution)/shard_map/ppermute | solution.py:283
  39.9 15.7 %collective-permute-start.9 = (bf16[8,1,2,64,128]{4,3,2,1,0:T(8,128)(2,1)S(1)}, bf16[8,1,2,64,128]{4,3,2,1,0:T(8,128)(2,1)S(1)}, u32[]{:S(2)}, u32[]{:S(2)}) collective-permute-start(bf16[8,1,2,64,128]{4,3,2,1,0:T(8,128)(2,1)S(1)} %get-tuple-element.44), channel_id=1, source_target_pairs={{0,4},{4,0},{8,12},{12,8},{16,20},{20,16},{24,28},{28,24},{1,5},{5... | collective-permute-start | bytes 786440 | tf_op jit(solution)/shard_map/ppermute | solution.py:289
  45.8 9.8 %collective-permute-start.10 = (bf16[8,1,2,64,128]{4,3,2,1,0:T(8,128)(2,1)S(1)}, bf16[8,1,2,64,128]{4,3,2,1,0:T(8,128)(2,1)S(1)}, u32[]{:S(2)}, u32[]{:S(2)}) collective-permute-start(bf16[8,1,2,64,128]{4,3,2,1,0:T(8,128)(2,1)S(1)} %add_convert_fusion.1), channel_id=1, source_target_pairs={{0,8},{4,28},{8,16},{12,4},{16,24},{20,12},{24,0},{28,20},{1,9},{5... | collective-permute-start | bytes 786440 | tf_op jit(solution)/shard_map/ppermute | solution.py:292

commit v6 on v5

--- a/solution.py
+++ b/solution.py
@@ -277,7 +277,7 @@
                 parts[-1][2] = lax.ppermute(merged, "energy", even_odd(2))
             relay, early = sums_of(c, (1, 2))
             if c > 0:
-                early, parts[-1][0] = lax.optimization_barrier((early, parts[-1][0]))
+                relay, early, parts[-1][0] = lax.optimization_barrier((relay, early, parts[-1][0]))
             near, late = sums_of(c, (0, 3))
             relay = lax.ppermute(relay, "energy", inner(1))
             early = lax.ppermute(early, "energy", even_odd(-2))

time: 57 us -> 56.9 us (level)
  Pallas kernels: 7.88 us -> 9.2 us
  waiting for transfers between devices: 26.1 us -> 24.8 us
    ppermute x2, starting transfers between devices: 4.04 us -> 5.77 us  [body(): early = lax.ppermute(early, 'energy', even_odd(-2))]
    ppermute x2, starting transfers between devices: 1.65 us -> 0.15 us  [body(): near = lax.ppermute(near, 'energy', inner(1))]
    pallas_call x4, Pallas kernels: 3.26 us -> 4.58 us  [atom_sums(): pl.pallas_call(functools.partial(gather_kernel, kinds, owner_count, capac...]
    ppermute x2, waiting for transfers between devices: 1.84 us -> 0.93 us  [body(): parts[-1][2] = lax.ppermute(merged, 'energy', even_odd(2))]
  transfers between devices with their start and end apart: 12 -> 12, of which waited for: 8 -> 8; matrix products, arithmetic and copies ran while one was open for 1% -> 1% of each run, Pallas kernels for 6% -> 8%
where the time goes in v6:
time: 56.9 us
  waiting for transfers between devices  24.8 us (44%)
  starting transfers between devices  19.8 us (35%)
  Pallas kernels  9.2 us (16%)
  other arithmetic  2.01 us (4%)
  local copies, waits for them, and re-layouts  0.95 us (2%)
    ppermute x2, waiting for transfers between devices, body(): near = lax.ppermute(near, 'energy', inner(1))  9.56 us
    ppermute x3, waiting for transfers between devices, to_owners(): lax.ppermute(blocks[d], 'atom', [(o, o ^ d) for o in range(owner_count)])  8.78 us
    ppermute x2, starting transfers between devices, body(): early = lax.ppermute(early, 'energy', even_odd(-2))  5.77 us
    ppermute x2, waiting for transfers between devices, body(): relay = lax.ppermute(relay, 'energy', inner(1))  5.32 us
    ppermute x2, starting transfers between devices, body(): relay = lax.ppermute(relay, 'energy', inner(1))  5.2 us
    pallas_call x1, Pallas kernels, bond_products(): pl.pallas_call(functools.partial(product_kernel, row_counts, capacity, sp...  4.62 us
    pallas_call x4, Pallas kernels, atom_sums(): pl.pallas_call(functools.partial(gather_kernel, kinds, owner_count, capac...  4.58 us
    all_to_all x1, starting transfers between devices, to_owners(): lax.all_to_all(blocks, 'atom', split_axis=0, concat_axis=0, tiled=True)  3.51 us
  transfers between devices with their start and end apart: 12, of which 8 were waited for; matrix products, arithmetic and copies ran while one was open for 1% of the time, Pallas kernels for 8%

profile of v6, /device:TPU:0, one launch (start us, length us, event | category | flops | bytes accessed | tf_op | source)
XLA Modules:
  0.0 56.9 jit_solution(8633791794536788308)
XLA Ops:
  0.0 0.7 %copy-done = s32[16]{0:T(128)S(1)} copy-done((s32[16]{0:T(128)S(1)}, s32[16]{0:T(128)}, u32[]{:S(2)}) %copy-start) | copy-done | bytes 88
  0.7 4.6 %bond_products.1 = (bf16[32,2,64,128]{3,2,1,0:T(8,128)(2,1)S(1)}, bf16[32,2,64,128]{3,2,1,0:T(8,128)(2,1)}) custom-call(s32[16]{0:T(128)S(1)} %copy-done, bf16[16,1,2,128,128]{4,3,2,1,0:T(8,128)(2,1)} %green_ref.1, bf16[16,3,2,128,128]{4,3,2,1,0:T(8,128)(2,1)} %coupling_ref.1), custom_call_target="tpu_custom_call" | custom-call | flops 1610612736 | bytes 4194304 | tf_op jit(solution)/shard_map/bond_products/pallas_call | solution.py:75
  5.3 0.2 convert_reduce_fusion
  5.9 3.0 %collective-permute-start.1 = (bf16[1040,128]{1,0:T(8,128)(2,1)S(1)}, bf16[1040,128]{1,0:T(8,128)(2,1)S(1)}, u32[]{:S(2)}, u32[]{:S(2)}) collective-permute-start(bf16[1040,128]{1,0:T(8,128)(2,1)S(1)} %get-tuple-element.54), channel_id=1, source_target_pairs={{0,2},{1,3},{2,0},{3,1},{4,6},{5,7},{6,4},{7,5},{8,10},{9,11},{10,... | collective-permute-start | bytes 798728 | tf_op jit(solution)/shard_map/ppermute | solution.py:250
  9.0 0.2 collective-permute-start
  9.1 3.5 %all-to-all-start = ((bf16[4,8,2,64,128]{4,3,2,1,0:T(8,128)(2,1)}), bf16[4,8,2,64,128]{4,3,2,1,0:T(8,128)(2,1)S(1)}, u32[]{:S(2)}, u32[]{:S(2)}) async-start(bf16[4,8,2,64,128]{4,3,2,1,0:T(8,128)(2,1)} %bitcast.16), calls=%async_computation | async-start | bytes 2097152 | tf_op jit(solution)/shard_map/all_to_all | solution.py:244
  12.7 3.5 %collective-permute-done.1.refs_2_ = bf16[1040,128]{1,0:T(8,128)(2,1)S(1)} collective-permute-done((bf16[1040,128]{1,0:T(8,128)(2,1)S(1)}, bf16[1040,128]{1,0:T(8,128)(2,1)S(1)}, u32[]{:S(2)}, u32[]{:S(2)}) %collective-permute-start.1) | collective-permute-done | bytes 266272 | tf_op jit(solution)/shard_map/ppermute | solution.py:250
  16.2 5.3 %collective-permute-done.2.refs_3_ = bf16[1040,128]{1,0:T(8,128)(2,1)S(1)} collective-permute-done((bf16[1040,128]{1,0:T(8,128)(2,1)S(1)}, bf16[1040,128]{1,0:T(8,128)(2,1)S(1)}, u32[]{:S(2)}, u32[]{:S(2)}) %collective-permute-start.2) | collective-permute-done | bytes 266272 | tf_op jit(solution)/shard_map/ppermute | solution.py:250
  21.9 1.1 %atom_sums.5 = (bf16[8,1,2,64,128]{4,3,2,1,0:T(8,128)(2,1)S(1)}, bf16[8,1,2,64,128]{4,3,2,1,0:T(8,128)(2,1)S(1)}) custom-call(s32[32]{0:T(128)S(1)} %add_reduce_fusion.atom_ref, f32[128]{0:T(128)S(1)} %reshape.49.weight_ref, bf16[1040,128]{1,0:T(8,128)(2,1)S(1)} %get-tuple-element.53.refs_0_, bf16[1040,128]{1,0:T(8,128)(2,1)S(1)} %collective-permute-done.refs_1_, ...), custom_call_target="tpu_custom_call" | custom-call | flops 2129920 | bytes 1064960 | tf_op jit(solution)/shard_map/atom_sums/pallas_call | solution.py:138
  23.0 1.6 %collective-permute-start.3 = (bf16[8,1,2,64,128]{4,3,2,1,0:T(8,128)(2,1)S(1)}, bf16[8,1,2,64,128]{4,3,2,1,0:T(8,128)(2,1)S(1)}, u32[]{:S(2)}, u32[]{:S(2)}) collective-permute-start(bf16[8,1,2,64,128]{4,3,2,1,0:T(8,128)(2,1)S(1)} %get-tuple-element.35), channel_id=1, source_target_pairs={{0,4},{4,0},{8,12},{12,8},{16,20},{20,16},{24,28},{28,24},{1,5},{5... | collective-permute-start | bytes 786440 | tf_op jit(solution)/shard_map/ppermute | solution.py:282
  24.6 3.6 %collective-permute-start.4 = (bf16[8,1,2,64,128]{4,3,2,1,0:T(8,128)(2,1)S(1)}, bf16[8,1,2,64,128]{4,3,2,1,0:T(8,128)(2,1)S(1)}, u32[]{:S(2)}, u32[]{:S(2)}) collective-permute-start(bf16[8,1,2,64,128]{4,3,2,1,0:T(8,128)(2,1)S(1)} %get-tuple-element.39), channel_id=1, source_target_pairs={{0,24},{4,12},{8,0},{12,20},{16,8},{20,28},{24,16},{28,4},{1,25},{... | collective-permute-start | bytes 786440 | tf_op jit(solution)/shard_map/ppermute | solution.py:283
  28.2 1.1 %atom_sums.4 = (bf16[8,1,2,64,128]{4,3,2,1,0:T(8,128)(2,1)S(1)}, f32[8,1,2,64,128]{4,3,2,1,0:T(8,128)S(1)}) custom-call(s32[32]{0:T(128)S(1)} %add_reduce_fusion.atom_ref, f32[128]{0:T(128)S(1)} %reshape.49.weight_ref, bf16[1040,128]{1,0:T(8,128)(2,1)S(1)} %get-tuple-element.53.refs_0_, bf16[1040,128]{1,0:T(8,128)(2,1)S(1)} %collective-permute-done.refs_1_, ...), custom_call_target="tpu_custom_call" | custom-call | flops 2129920 | bytes 1064960 | tf_op jit(solution)/shard_map/atom_sums/pallas_call | solution.py:138
  29.4 2.6 %collective-permute-done.3 = bf16[8,1,2,64,128]{4,3,2,1,0:T(8,128)(2,1)S(1)} collective-permute-done((bf16[8,1,2,64,128]{4,3,2,1,0:T(8,128)(2,1)S(1)}, bf16[8,1,2,64,128]{4,3,2,1,0:T(8,128)(2,1)S(1)}, u32[]{:S(2)}, u32[]{:S(2)}) %collective-permute-start.3) | collective-permute-done | bytes 262176 | tf_op jit(solution)/shard_map/ppermute | solution.py:282
  32.1 0.2 all-to-all-done
  32.3 1.8 %collective-permute-start.6 = (bf16[8,1,2,64,128]{4,3,2,1,0:T(8,128)(2,1)S(1)}, bf16[8,1,2,64,128]{4,3,2,1,0:T(8,128)(2,1)S(1)}, u32[]{:S(2)}, u32[]{:S(2)}) collective-permute-start(bf16[8,1,2,64,128]{4,3,2,1,0:T(8,128)(2,1)S(1)} %add_convert_fusion.3), channel_id=1, source_target_pairs={{0,8},{4,28},{8,16},{12,4},{16,24},{20,12},{24,0},{28,20},{1,9},{5... | collective-permute-start | bytes 786440 | tf_op jit(solution)/shard_map/ppermute | solution.py:277
  34.1 1.1 %atom_sums.6 = (bf16[8,1,2,64,128]{4,3,2,1,0:T(8,128)(2,1)S(1)}, bf16[8,1,2,64,128]{4,3,2,1,0:T(8,128)(2,1)S(1)}) custom-call(s32[32]{0:T(128)S(1)} %add_reduce_fusion.atom_ref, f32[128]{0:T(128)S(1)} %reshape.49.weight_ref, bf16[4096,128]{1,0:T(8,128)(2,1)S(1)} %bitcast.30), custom_call_target="tpu_custom_call" | custom-call | flops 2097152 | bytes 1048576 | tf_op jit(solution)/shard_map/atom_sums/pallas_call | solution.py:138
  35.3 3.6 %collective-permute-start.5 = (bf16[8,1,2,64,128]{4,3,2,1,0:T(8,128)(2,1)S(1)}, bf16[8,1,2,64,128]{4,3,2,1,0:T(8,128)(2,1)S(1)}, u32[]{:S(2)}, u32[]{:S(2)}) collective-permute-start(bf16[8,1,2,64,128]{4,3,2,1,0:T(8,128)(2,1)S(1)} %get-tuple-element.40), channel_id=1, source_target_pairs={{0,4},{4,0},{8,12},{12,8},{16,20},{20,16},{24,28},{28,24},{1,5},{5... | collective-permute-start | bytes 786440 | tf_op jit(solution)/shard_map/ppermute | solution.py:282
  39.0 2.2 %collective-permute-start.8 = (bf16[8,1,2,64,128]{4,3,2,1,0:T(8,128)(2,1)S(1)}, bf16[8,1,2,64,128]{4,3,2,1,0:T(8,128)(2,1)S(1)}, u32[]{:S(2)}, u32[]{:S(2)}) collective-permute-start(bf16[8,1,2,64,128]{4,3,2,1,0:T(8,128)(2,1)S(1)} %get-tuple-element.45), channel_id=1, source_target_pairs={{0,24},{4,12},{8,0},{12,20},{16,8},{20,28},{24,16},{28,4},{1,25},{... | collective-permute-start | bytes 786440 | tf_op jit(solution)/shard_map/ppermute | solution.py:283
  41.1 1.2 %atom_sums.7 = (bf16[8,1,2,64,128]{4,3,2,1,0:T(8,128)(2,1)S(1)}, f32[8,1,2,64,128]{4,3,2,1,0:T(8,128)S(1)}) custom-call(s32[32]{0:T(128)S(1)} %add_reduce_fusion.atom_ref, f32[128]{0:T(128)S(1)} %reshape.49.weight_ref, bf16[4096,128]{1,0:T(8,128)(2,1)S(1)} %bitcast.31), custom_call_target="tpu_custom_call" | custom-call | flops 2097152 | bytes 1048576 | tf_op jit(solution)/shard_map/atom_sums/pallas_call | solution.py:138
  42.4 0.9 %collective-permute-done.6 = bf16[8,1,2,64,128]{4,3,2,1,0:T(8,128)(2,1)S(1)} collective-permute-done((bf16[8,1,2,64,128]{4,3,2,1,0:T(8,128)(2,1)S(1)}, bf16[8,1,2,64,128]{4,3,2,1,0:T(8,128)(2,1)S(1)}, u32[]{:S(2)}, u32[]{:S(2)}) %collective-permute-start.6) | collective-permute-done | bytes 262176 | tf_op jit(solution)/shard_map/ppermute | solution.py:277
  43.4 2.7 %collective-permute-done.5 = bf16[8,1,2,64,128]{4,3,2,1,0:T(8,128)(2,1)S(1)} collective-permute-done((bf16[8,1,2,64,128]{4,3,2,1,0:T(8,128)(2,1)S(1)}, bf16[8,1,2,64,128]{4,3,2,1,0:T(8,128)(2,1)S(1)}, u32[]{:S(2)}, u32[]{:S(2)}) %collective-permute-start.5) | collective-permute-done | bytes 262176 | tf_op jit(solution)/shard_map/ppermute | solution.py:282
  46.3 5.4 %collective-permute-done.7 = bf16[8,1,2,64,128]{4,3,2,1,0:T(8,128)(2,1)S(1)} collective-permute-done((bf16[8,1,2,64,128]{4,3,2,1,0:T(8,128)(2,1)S(1)}, bf16[8,1,2,64,128]{4,3,2,1,0:T(8,128)(2,1)S(1)}, u32[]{:S(2)}, u32[]{:S(2)}) %collective-permute-start.7) | collective-permute-done | bytes 262176 | tf_op jit(solution)/shard_map/ppermute | solution.py:289
  51.8 4.1 %collective-permute-done.9 = bf16[8,1,2,64,128]{4,3,2,1,0:T(8,128)(2,1)S(1)} collective-permute-done((bf16[8,1,2,64,128]{4,3,2,1,0:T(8,128)(2,1)S(1)}, bf16[8,1,2,64,128]{4,3,2,1,0:T(8,128)(2,1)S(1)}, u32[]{:S(2)}, u32[]{:S(2)}) %collective-permute-start.9) | collective-permute-done | bytes 262176 | tf_op jit(solution)/shard_map/ppermute | solution.py:289
  56.1 0.8 %pad_maximum_fusion = bf16[8,1,2,128,128]{4,3,2,1,0:T(8,128)(2,1)} fusion(bf16[8,1,2,64,128]{4,3,2,1,0:T(8,128)(2,1)S(1)} %add_convert_fusion, bf16[8,1,2,64,128]{4,3,2,1,0:T(8,128)(2,1)S(1)} %add_convert_fusion.2), kind=kLoop, calls=%fused_computation.6 | loop fusion | flops 1048576 | bytes 1048576 | tf_op jit(solution)/shard_map/concatenate | solution.py:308
  (37 shorter events, 1.6 us)
Async XLA Ops:
  0.0 0.7 %copy-start = (s32[16]{0:T(128)S(1)}, s32[16]{0:T(128)}, u32[]{:S(2)}) copy-start(s32[16]{0:T(128)} %atom_ref.1) | copy-start | bytes 196
  0.7 4.9 %copy-start.1 = (f32[2,16,2]{1,2,0:T(2,128)S(1)}, f32[2,16,2]{1,2,0:T(2,128)}, u32[]{:S(2)}) copy-start(f32[2,16,2]{1,2,0:T(2,128)} %param.7) | copy-start | bytes 772
  0.7 4.9 %copy-start.2 = (s32[16,2]{0,1:T(2,128)S(1)}, s32[16,2]{0,1:T(2,128)}, u32[]{:S(2)}) copy-start(s32[16,2]{0,1:T(2,128)} %param.8) | copy-start | bytes 388
  5.9 10.2 %collective-permute-start.1 = (bf16[1040,128]{1,0:T(8,128)(2,1)S(1)}, bf16[1040,128]{1,0:T(8,128)(2,1)S(1)}, u32[]{:S(2)}, u32[]{:S(2)}) collective-permute-start(bf16[1040,128]{1,0:T(8,128)(2,1)S(1)} %get-tuple-element.54), channel_id=1, source_target_pairs={{0,2},{1,3},{2,0},{3,1},{4,6},{5,7},{6,4},{7,5},{8,10},{9,11},{10,... | collective-permute-start | bytes 798728 | tf_op jit(solution)/shard_map/ppermute | solution.py:250
  8.9 12.5 %collective-permute-start.2 = (bf16[1040,128]{1,0:T(8,128)(2,1)S(1)}, bf16[1040,128]{1,0:T(8,128)(2,1)S(1)}, u32[]{:S(2)}, u32[]{:S(2)}) collective-permute-start(bf16[1040,128]{1,0:T(8,128)(2,1)S(1)} %get-tuple-element.55), channel_id=1, source_target_pairs={{0,3},{1,2},{2,1},{3,0},{4,7},{5,6},{6,5},{7,4},{8,11},{9,10},{10,... | collective-permute-start | bytes 798728 | tf_op jit(solution)/shard_map/ppermute | solution.py:250
  9.0 12.5 %collective-permute-start = (bf16[1040,128]{1,0:T(8,128)(2,1)S(1)}, bf16[1040,128]{1,0:T(8,128)(2,1)S(1)}, u32[]{:S(2)}, u32[]{:S(2)}) collective-permute-start(bf16[1040,128]{1,0:T(8,128)(2,1)S(1)} %get-tuple-element.56), channel_id=1, source_target_pairs={{0,1},{1,0},{2,3},{3,2},{4,5},{5,4},{6,7},{7,6},{8,9},{9,8},{10,11... | collective-permute-start | bytes 798728 | tf_op jit(solution)/shard_map/ppermute | solution.py:250
  9.1 23.1 %all-to-all-start = ((bf16[4,8,2,64,128]{4,3,2,1,0:T(8,128)(2,1)}), bf16[4,8,2,64,128]{4,3,2,1,0:T(8,128)(2,1)S(1)}, u32[]{:S(2)}, u32[]{:S(2)}) async-start(bf16[4,8,2,64,128]{4,3,2,1,0:T(8,128)(2,1)} %bitcast.16), calls=%async_computation | async-start | bytes 2097152 | tf_op jit(solution)/shard_map/all_to_all | solution.py:244
  23.0 8.9 %collective-permute-start.3 = (bf16[8,1,2,64,128]{4,3,2,1,0:T(8,128)(2,1)S(1)}, bf16[8,1,2,64,128]{4,3,2,1,0:T(8,128)(2,1)S(1)}, u32[]{:S(2)}, u32[]{:S(2)}) collective-permute-start(bf16[8,1,2,64,128]{4,3,2,1,0:T(8,128)(2,1)S(1)} %get-tuple-element.35), channel_id=1, source_target_pairs={{0,4},{4,0},{8,12},{12,8},{16,20},{20,16},{24,28},{28,24},{1,5},{5... | collective-permute-start | bytes 786440 | tf_op jit(solution)/shard_map/ppermute | solution.py:282
  24.6 10.6 %collective-permute-start.4 = (bf16[8,1,2,64,128]{4,3,2,1,0:T(8,128)(2,1)S(1)}, bf16[8,1,2,64,128]{4,3,2,1,0:T(8,128)(2,1)S(1)}, u32[]{:S(2)}, u32[]{:S(2)}) collective-permute-start(bf16[8,1,2,64,128]{4,3,2,1,0:T(8,128)(2,1)S(1)} %get-tuple-element.39), channel_id=1, source_target_pairs={{0,24},{4,12},{8,0},{12,20},{16,8},{20,28},{24,16},{28,4},{1,25},{... | collective-permute-start | bytes 786440 | tf_op jit(solution)/shard_map/ppermute | solution.py:283
  32.3 11.0 %collective-permute-start.6 = (bf16[8,1,2,64,128]{4,3,2,1,0:T(8,128)(2,1)S(1)}, bf16[8,1,2,64,128]{4,3,2,1,0:T(8,128)(2,1)S(1)}, u32[]{:S(2)}, u32[]{:S(2)}) collective-permute-start(bf16[8,1,2,64,128]{4,3,2,1,0:T(8,128)(2,1)S(1)} %add_convert_fusion.3), channel_id=1, source_target_pairs={{0,8},{4,28},{8,16},{12,4},{16,24},{20,12},{24,0},{28,20},{1,9},{5... | collective-permute-start | bytes 786440 | tf_op jit(solution)/shard_map/ppermute | solution.py:277
  35.3 10.8 %collective-permute-start.5 = (bf16[8,1,2,64,128]{4,3,2,1,0:T(8,128)(2,1)S(1)}, bf16[8,1,2,64,128]{4,3,2,1,0:T(8,128)(2,1)S(1)}, u32[]{:S(2)}, u32[]{:S(2)}) collective-permute-start(bf16[8,1,2,64,128]{4,3,2,1,0:T(8,128)(2,1)S(1)} %get-tuple-element.40), channel_id=1, source_target_pairs={{0,4},{4,0},{8,12},{12,8},{16,20},{20,16},{24,28},{28,24},{1,5},{5... | collective-permute-start | bytes 786440 | tf_op jit(solution)/shard_map/ppermute | solution.py:282
  38.9 12.8 %collective-permute-start.7 = (bf16[8,1,2,64,128]{4,3,2,1,0:T(8,128)(2,1)S(1)}, bf16[8,1,2,64,128]{4,3,2,1,0:T(8,128)(2,1)S(1)}, u32[]{:S(2)}, u32[]{:S(2)}) collective-permute-start(bf16[8,1,2,64,128]{4,3,2,1,0:T(8,128)(2,1)S(1)} %get-tuple-element.44), channel_id=1, source_target_pairs={{0,4},{4,0},{8,12},{12,8},{16,20},{20,16},{24,28},{28,24},{1,5},{5... | collective-permute-start | bytes 786440 | tf_op jit(solution)/shard_map/ppermute | solution.py:289
  39.0 12.8 %collective-permute-start.8 = (bf16[8,1,2,64,128]{4,3,2,1,0:T(8,128)(2,1)S(1)}, bf16[8,1,2,64,128]{4,3,2,1,0:T(8,128)(2,1)S(1)}, u32[]{:S(2)}, u32[]{:S(2)}) collective-permute-start(bf16[8,1,2,64,128]{4,3,2,1,0:T(8,128)(2,1)S(1)} %get-tuple-element.45), channel_id=1, source_target_pairs={{0,24},{4,12},{8,0},{12,20},{16,8},{20,28},{24,16},{28,4},{1,25},{... | collective-permute-start | bytes 786440 | tf_op jit(solution)/shard_map/ppermute | solution.py:283
  42.3 13.6 %collective-permute-start.9 = (bf16[8,1,2,64,128]{4,3,2,1,0:T(8,128)(2,1)S(1)}, bf16[8,1,2,64,128]{4,3,2,1,0:T(8,128)(2,1)S(1)}, u32[]{:S(2)}, u32[]{:S(2)}) collective-permute-start(bf16[8,1,2,64,128]{4,3,2,1,0:T(8,128)(2,1)S(1)} %get-tuple-element.46), channel_id=1, source_target_pairs={{0,4},{4,0},{8,12},{12,8},{16,20},{20,16},{24,28},{28,24},{1,5},{5... | collective-permute-start | bytes 786440 | tf_op jit(solution)/shard_map/ppermute | solution.py:289
  46.2 9.8 %collective-permute-start.10 = (bf16[8,1,2,64,128]{4,3,2,1,0:T(8,128)(2,1)S(1)}, bf16[8,1,2,64,128]{4,3,2,1,0:T(8,128)(2,1)S(1)}, u32[]{:S(2)}, u32[]{:S(2)}) collective-permute-start(bf16[8,1,2,64,128]{4,3,2,1,0:T(8,128)(2,1)S(1)} %add_convert_fusion.1), channel_id=1, source_target_pairs={{0,8},{4,28},{8,16},{12,4},{16,24},{20,12},{24,0},{28,20},{1,9},{5... | collective-permute-start | bytes 786440 | tf_op jit(solution)/shard_map/ppermute | solution.py:292
